TPU v7x, 32 devices: a whole 2x2x4 slice. The times are simulated.
32 devices in a mesh: section: 2 (over x), dp: 4 (over y, core), mp: 4 (over z).
Axes of the slice: x: 2, y: 2, z: 4, core: 2. Of those that a mesh axis runs over, the one named last changes fastest.
Arguments:
- hidden: bfloat16 [2, 4, 256, 5120], P('section', 'dp'), may hold values from -6 to 6
- gain: float32 [2, 5120], P('section'), may hold values from 0.5 to 2
- w_first: bfloat16 [2, 5120, 2560], P('section', 'dp', 'mp'), may hold values from -0.078125 to 0.078125
- w_second: bfloat16 [2, 5120, 2560], P('section', 'dp', 'mp'), may hold values from -0.078125 to 0.078125
- lengths: int32 [4, 2], P('dp'), may hold values from 32 to 256, as said below
- cotangent: bfloat16 [2, 4, 256, 5120], P('section', 'dp'), may hold values from -6 to 6
Outputs:
- result: bfloat16 [2, 4, 256, 5120], P('section', 'dp')
- d_hidden: bfloat16 [2, 4, 256, 5120], P('section', 'dp')
- d_gain: float32 [2, 5120], P('section', 'dp')
- d_first: float32 [2, 5120, 2560], P('section', 'dp', 'mp')
- d_second: float32 [2, 5120, 2560], P('section', 'dp', 'mp')
Inputs may be any that keep to these rules, and one draw needn't show every extreme that they name: `lengths`: each row's source count and target count; positions at or past a count are padding.
All inputs are finite; a program needn't handle non-finite values.
Results may differ from a plain program's by a relative error of at most 0.017.
Values may be sent and summed in bfloat16 or wider, within the bound.
No kernel may reach another device: no remote copies, remote signals or barrier semaphores. Data moves between devices by JAX's collectives and lax.ppermute only.
A program may use at most 128 MiB of HBM per device.

v0:
```python
import functools
import math

import jax
import jax.numpy as jnp
from jax import lax
from jax.experimental import pallas as pl
from jax.experimental.pallas import tpu as pltpu
from jax.sharding import PartitionSpec as P

HEAD = 128
EPS = 1e-06
MASKED = -1e30
WAIT = 12 * 10**9
CORES = 2
F32 = jnp.float32
BF16 = jnp.bfloat16


def dot_rows(left, right):
    return lax.dot_general(left, right, (((0,), (0,)), ((), ())), preferred_element_type=F32)


def dot_last(left, right):
    return lax.dot_general(left, right, (((1,), (1,)), ((), ())), preferred_element_type=F32)


def dot_plain(left, right):
    return jnp.dot(left, right, preferred_element_type=F32)


BOTH, ENCODER, DECODER = (0, 1), (0,), (1,)


def permute(x, axis, to, sections):
    n = lax.axis_size(axis)
    if sections == BOTH:
        return lax.ppermute(x, axis, [(i, to(i, n)) for i in range(n)])
    pairs = [(s * n + i, s * n + to(i, n)) for s in sections for i in range(n)]
    return lax.ppermute(x, ("section", axis), pairs)


def core_swap(x, sections=BOTH):
    return permute(x, "dp", lambda i, n: i ^ 1, sections)


def chip_shift(x, by, sections=BOTH):
    return permute(x, "dp", lambda i, n: (i + by * CORES) % n, sections)


def home_shift(x, by):
    n = lax.axis_size("dp")
    pairs = [(n + i, (i + by * CORES) % n) for i in range(n)]
    return lax.ppermute(x, ("section", "dp"), pairs)


def head_shift(x, by, sections=BOTH):
    return permute(x, "mp", lambda i, n: (i + by) % n, sections)


ANYWHERE = pl.BlockSpec(memory_space=pl.ANY)


def add_kernel(place_ref, got_ref, part_ref, *refs):
    refs[-1][...] = (got_ref[...].astype(F32) + part_ref[...].astype(F32)).astype(refs[-1].dtype)


def add_block(got, parts, place, dtype, *before):
    seqs, tokens, features = got.shape
    steps = 2 if features % 256 == 0 else 1
    piece = features // steps
    block = pl.BlockSpec((seqs, tokens, piece), lambda i, at: (0, 0, i))
    return pl.pallas_call(
        add_kernel,
        grid_spec=pltpu.PrefetchScalarGridSpec(
            num_scalar_prefetch=1,
            grid=(steps,),
            in_specs=[
                block,
                pl.BlockSpec((seqs, tokens, piece), lambda i, at: (0, at[0], i)),
            ]
            + [ANYWHERE] * len(before),
            out_specs=block,
        ),
        out_shape=jax.ShapeDtypeStruct(got.shape, dtype),
        compiler_params=pltpu.CompilerParams(vmem_limit_bytes=32 * 2**20),
        cost_estimate=pl.CostEstimate(flops=WAIT, bytes_accessed=0, transcendentals=0),
        name="add_block",
    )(place.reshape(1), got, parts, *before)


def place_kernel(place_ref, rows_ref, other_ref, *refs):
    refs[-1][...] = jnp.where(place_ref[1] == 1, rows_ref[...], other_ref[...])


def place_block(whole, length, rows, place, other, wanted, *before):
    tokens, features = rows.shape
    steps = 2 if features % 256 == 0 else 1
    piece = features // steps
    where = jnp.stack([place, wanted.astype(jnp.int32)])
    block = pl.BlockSpec((tokens, piece), lambda i, at: (at[0], i))
    mine = pl.BlockSpec((tokens, piece), lambda i, at: (0, i))
    whole = [] if whole is None else [whole]
    if other is None:
        other, other_block = rows, mine
    else:
        other_block = block
    return pl.pallas_call(
        place_kernel,
        grid_spec=pltpu.PrefetchScalarGridSpec(
            num_scalar_prefetch=1,
            grid=(steps,),
            in_specs=[mine, other_block] + [ANYWHERE] * len(whole + list(before)),
            out_specs=block,
        ),
        out_shape=jax.ShapeDtypeStruct((length, features), rows.dtype),
        input_output_aliases={3: 0} if whole else {},
        compiler_params=pltpu.CompilerParams(vmem_limit_bytes=32 * 2**20),
        cost_estimate=pl.CostEstimate(flops=WAIT, bytes_accessed=0, transcendentals=0),
        name="place_block",
    )(where, rows, other, *whole, *before)


def pass_kernel(rows_ref, *refs):
    refs[-1][...] = rows_ref[...]


def pass_on(rows, *before):
    block = pl.BlockSpec(rows.shape, lambda i: (0, 0))
    return pl.pallas_call(
        pass_kernel,
        grid=(1,),
        in_specs=[block] + [ANYWHERE] * len(before),
        out_specs=block,
        out_shape=jax.ShapeDtypeStruct(rows.shape, rows.dtype),
        compiler_params=pltpu.CompilerParams(vmem_limit_bytes=32 * 2**20),
        cost_estimate=pl.CostEstimate(flops=10**9, bytes_accessed=0, transcendentals=0),
        name="pass_on",
    )(rows, *before)


def join_kernel(count, *refs):
    at = 0
    for ref in refs[:count]:
        refs[-1][:, at : at + ref.shape[1]] = ref[...]
        at += ref.shape[1]


def join(parts, *before):
    rows = parts[0].shape[0]
    steps = 2 if rows % 32 == 0 else 1
    width = sum(p.shape[1] for p in parts)

    def block(columns):
        return pl.BlockSpec((rows // steps, columns), lambda i: (i, 0))

    return pl.pallas_call(
        functools.partial(join_kernel, len(parts)),
        grid=(steps,),
        in_specs=[block(p.shape[1]) for p in parts] + [ANYWHERE] * len(before),
        out_specs=block(width),
        out_shape=jax.ShapeDtypeStruct((rows, width), parts[0].dtype),
        compiler_params=pltpu.CompilerParams(vmem_limit_bytes=32 * 2**20),
        cost_estimate=pl.CostEstimate(flops=10**9, bytes_accessed=0, transcendentals=0),
        name="join",
    )(*parts, *before)


def attention_kernel(lengths_ref, q_ref, kv_ref, g_ref, ctx_ref, gq_ref, gkv_ref):
    scale = 1.0 / math.sqrt(HEAD)
    q, k, v, g = q_ref[...], kv_ref[0], kv_ref[1], g_ref[...]
    scores = dot_last(q, k) * scale
    column = lax.broadcasted_iota(jnp.int32, scores.shape, 1)
    scores = jnp.where(column < lengths_ref[0, 0], scores, MASKED)
    top = jnp.max(scores, axis=-1, keepdims=True)
    raised = jnp.exp(scores - top)
    weights = raised / jnp.sum(raised, axis=-1, keepdims=True)
    low = weights.astype(BF16)
    ctx_ref[...] = dot_plain(low, v).astype(BF16)
    gkv_ref[1] = dot_rows(low, g).astype(BF16)
    grad_weights = dot_last(g, v)
    centered = grad_weights - jnp.sum(weights * grad_weights, axis=-1, keepdims=True)
    grad_scores = (weights * centered * scale).astype(BF16)
    gq_ref[...] = dot_plain(grad_scores, k).astype(BF16)
    gkv_ref[0] = dot_rows(grad_scores, q).astype(BF16)


def attention(lengths, q, kv, g):
    rows, columns = q.shape
    block = pl.BlockSpec((rows, HEAD), lambda h: (0, h))
    pair = pl.BlockSpec((2, rows, HEAD), lambda h: (0, 0, h))
    shape = jax.ShapeDtypeStruct((rows, columns), BF16)
    heads = columns // HEAD
    return pl.pallas_call(
        attention_kernel,
        grid=(heads,),
        in_specs=[pl.BlockSpec(memory_space=pltpu.SMEM), block, pair, block],
        out_specs=[block, block, pair],
        out_shape=[shape, shape, jax.ShapeDtypeStruct((2, rows, columns), BF16)],
        compiler_params=pltpu.CompilerParams(vmem_limit_bytes=32 * 2**20),
        cost_estimate=pl.CostEstimate(
            flops=14 * rows * rows * columns,
            bytes_accessed=16 * rows * columns,
            transcendentals=heads * rows * rows,
        ),
        name="attention",
    )(lengths, q, kv, g)


def shards(hidden, gain, w_first, w_second, lengths, cotangent):
    encoder = lax.axis_index("section") == 0
    place = lax.axis_index("dp")
    chip, core = place // CORES, lax.rem(place, CORES)
    head_place = lax.axis_index("mp")
    heads_axis = lax.axis_size("mp")
    chips = lax.axis_size("dp") // CORES
    states = hidden[0, 0]
    length, width = states.shape
    gains = gain[0][None, :]
    tile = w_first.shape[1]
    span = CORES * tile
    columns = w_first.shape[2]
    block = length // heads_axis
    others = range(1, chips)

    def chip_at(k):
        return lax.rem(chip + k + chips, chips)

    def chip_columns(array, k):
        return lax.dynamic_slice_in_dim(array, chip_at(k) * span, span, 1)

    def in_order(own, other):
        ahead = [jnp.where(core == 0, a, b) for a, b in zip(own, other)]
        behind = [jnp.where(core == 0, b, a) for a, b in zip(own, other)]
        return jnp.concatenate(ahead + behind, axis=0)

    def whole_chip(own):
        return in_order([own], [core_swap(own)])

    first, second = w_first[0], w_second[0]
    first_far = [chip_shift(first, k, DECODER) for k in others]
    far_states = [chip_shift(chip_columns(states, k), k, ENCODER) for k in others]
    first_chip = whole_chip(first)
    second_chip = whole_chip(second)
    wide = states.astype(F32)
    inverse = lax.rsqrt(jnp.mean(wide * wide, axis=-1, keepdims=True) + EPS)
    inverse_row = inverse.reshape(1, length)
    far_inverse = [chip_shift(inverse_row, k, ENCODER).reshape(length, 1) for k in others]
    unit = wide * inverse
    normed = (unit * gains).astype(BF16)
    keep = jnp.arange(length)[:, None] < lengths[0, 1]
    grad_out = jnp.where(keep, cotangent[0, 0], jnp.zeros((), BF16))

    near_normed = chip_columns(normed, 0)
    second_left = jnp.where(encoder, near_normed, chip_columns(grad_out, 0))
    own_first = dot_plain(near_normed, first_chip)
    own_second = dot_plain(second_left, second_chip)
    normed_columns = [chip_columns(normed, -k) for k in others]
    grad_columns = [chip_columns(grad_out, -k) for k in others]
    far_states, own_first, own_second, normed_columns, grad_columns = lax.optimization_barrier(
        (far_states, own_first, own_second, normed_columns, grad_columns)
    )
    gains_chip = chip_columns(gains, 0)
    far_normed = [
        (rows.astype(F32) * inv * gains_chip).astype(BF16)
        for rows, inv in zip(far_states, far_inverse)
    ]

    both = jnp.stack([own_first, own_second])
    for k in others:
        part = jnp.stack(
            [dot_plain(far_normed[k - 1], w).astype(BF16) for w in (first_chip, second_chip)]
        )
        both = both + chip_shift(part, -k, ENCODER).astype(F32)
    both, first_far = lax.optimization_barrier((both.astype(BF16), first_far))
    second_far = [chip_shift(second, k, DECODER) for k in others]
    memory_heads = lax.ppermute(both, "section", [(0, 1)])

    first_far = [whole_chip(w) for w in first_far]
    queries, grad_context = own_first, own_second
    for k in others:
        queries = queries + dot_plain(normed_columns[k - 1], first_far[k - 1])
    queries = queries.astype(BF16)
    memory_heads, second_far, queries = lax.optimization_barrier(
        (memory_heads, second_far, queries)
    )
    second_far = [whole_chip(w) for w in second_far]
    for k in others:
        grad_context = grad_context + dot_plain(grad_columns[k - 1], second_far[k - 1])
    grad_context = grad_context.astype(BF16)
    context, grad_query, grad_memory = attention(lengths, queries, memory_heads, grad_context)
    grad_memory, *far_memory = [home_shift(grad_memory, k) for k in range(chips)]

    def block_at(array, place):
        at = lax.rem(place + 2 * heads_axis, heads_axis) * block
        return lax.dynamic_slice_in_dim(array, at, block, array.ndim - 2)

    def first_block(parts):
        return block_at(parts, head_place - 1)

    def summed(got, parts, step):
        return got.astype(F32) + block_at(parts, head_place - 2 - step).astype(F32)

    def my_rows(array):
        return block_at(array, head_place)

    def place_rows(whole, rows, step, column=0):
        at = lax.rem(head_place - step + heads_axis, heads_axis) * block
        return lax.dynamic_update_slice(whole, rows, (at, column))

    def piled(parts):
        return jnp.stack([p.astype(BF16) for p in parts])

    last = heads_axis - 1
    def send_out(x):
        return head_shift(x, 1, DECODER)

    def send_memory(x):
        return head_shift(x, 1, ENCODER)

    def whole_rows(pieces):
        whole = jnp.zeros((block, width), F32)
        for k in range(chips):
            whole = lax.dynamic_update_slice_in_dim(whole, pieces[k], chip_at(-k) * span, 1)
        return whole

    back_parts = piled(dot_last(grad_query, w) for w in [first_chip] + first_far)
    back_held = first_block(back_parts)
    back_got = send_out(back_held)
    out_parts = piled(dot_last(context, w) for w in [second_chip] + second_far)
    out_held = first_block(out_parts)
    out_got = send_out(out_held)
    memory_parts = piled(
        dot_last(g[0], first_chip) + dot_last(g[1], second_chip)
        for g in [grad_memory] + far_memory
    )
    memory_held = first_block(memory_parts)
    memory_got = send_memory(memory_held)

    def at(step):
        return lax.rem(head_place + 2 * heads_axis - step, heads_axis)

    for step in range(last):
        kind = BF16 if step < last - 1 else F32
        back_held = add_block(back_got, back_parts, at(2 + step), kind, out_held)
        if step == 0:
            moved = []
            for k in others:
                parts = [chip_columns(normed, k), chip_columns(grad_out, k), grad_query, context]
                moved.append(chip_shift(join(parts, back_held), k, DECODER))
        if step < last - 1:
            back_got = send_out(back_held)
            out_held = add_block(out_got, out_parts, at(2 + step), kind, back_held)
            out_got = send_out(out_held)
        memory_held = add_block(memory_got, memory_parts, at(2 + step), kind, back_held)
        if step < last - 1:
            memory_got = send_memory(memory_held)
    back_sum, memory_sum = back_held, memory_held

    homes = [chip_shift(memory_sum[k].astype(BF16), -k, ENCODER).astype(F32) for k in others]
    grad_normed = whole_rows(
        [jnp.where(encoder, memory_sum[0], back_sum[0])]
        + [jnp.where(encoder, homes[chips - 1 - k], back_sum[k]) for k in others]
    )
    grad_normed = grad_normed + jnp.where(encoder, my_rows(cotangent[0, 0]).astype(F32), 0.0)
    my_inverse = my_rows(inverse)
    my_unit = my_rows(states).astype(F32) * my_inverse
    residual = jnp.where(encoder, 0.0, my_rows(grad_out).astype(F32))
    scaled = grad_normed * gains
    inner = jnp.mean(scaled * my_unit, axis=-1, keepdims=True)
    grad_rows = (my_inverse * (scaled - my_unit * inner) + residual).astype(BF16)

    back_held = grad_rows
    back_got = head_shift(back_held, 1)
    gain_part = jnp.sum(grad_normed * my_unit, axis=0, keepdims=True)
    gain_parts = [head_shift(gain_part, k) for k in range(1, heads_axis)]
    out_sum = add_block(out_got, out_parts, at(1 + last), F32, back_held)
    out_held = (my_rows(states).astype(F32) + whole_rows(out_sum)).astype(BF16)
    out_got = send_out(out_held)
    arrivals = [(out_held, back_held)]

    decoder, always = ~encoder, jnp.bool_(True)

    def place_grad(whole, rows, step, *before):
        return place_block(whole, length, rows, at(step), None, always, *before)

    def place_out(whole, rows, step, *before):
        return place_block(whole, length, rows, at(step), normed, decoder, *before)

    def next_round(step, back_got, out_got, grad_states, result, first, then):
        arrived = back_got
        if step < last:
            back_got = head_shift(arrived, 1)
        grad_states = place_grad(grad_states, arrived, step, result, *first)
        arrived = out_got
        if step < last:
            out_got = send_out(arrived)
        result = place_out(result, arrived, step, grad_states, *then)
        return back_got, out_got, grad_states, result

    arrived = back_got
    back_got = head_shift(arrived, 1)
    grad_states = place_grad(None, arrived, 1, out_held)
    arrived = out_got
    out_got = send_out(arrived)
    result = place_out(None, arrived, 1, grad_states)
    grad_states = place_grad(grad_states, back_held, 0, result)
    result = place_out(result, out_held, 0, grad_states)
    for part in gain_parts:
        gain_part = gain_part + part
    gain_part = pass_on(gain_part, back_got)
    gain_chip = chip_columns(gain_part, 0)
    gain_far = [chip_shift(chip_columns(gain_part, k), k) for k in others]
    left, right = [near_normed], [second_left]
    grads_first = [jnp.where(encoder, grad_memory[0], grad_query)]
    grads_second = [jnp.where(encoder, grad_memory[1], context)]
    for k in others:
        pieces = jnp.split(moved[k - 1], (span, 2 * span, 2 * span + columns), axis=1)
        left.append(jnp.where(encoder, far_normed[k - 1], pieces[0]))
        right.append(jnp.where(encoder, far_normed[k - 1], pieces[1]))
        grads_first.append(jnp.where(encoder, far_memory[k - 1][0], pieces[2]))
        grads_second.append(jnp.where(encoder, far_memory[k - 1][1], pieces[3]))

    def weight_grads(half):
        def one(rows, grads):
            rows, grads = jnp.concatenate(rows, axis=0), jnp.concatenate(grads, axis=0)
            return dot_rows(lax.dynamic_slice_in_dim(rows, half * tile, tile, 1), grads)

        return one(left, grads_first), one(right, grads_second)

    halves = jnp.stack([x.astype(BF16) for x in weight_grads(1 - core)])
    swapped = core_swap(halves)
    for step in range(2, last):
        back_got, out_got, grad_states, result = next_round(
            step, back_got, out_got, grad_states, result, [gain_part], [halves]
        )
    for part in gain_far:
        gain_chip = gain_chip + part
    gain_sum = lax.dynamic_slice_in_dim(gain_chip, core * tile, tile, 1)
    gain_sum = gain_sum + core_swap(
        lax.dynamic_slice_in_dim(gain_chip, (1 - core) * tile, tile, 1)
    )
    first_sum, second_sum = weight_grads(core)
    first_sum = first_sum + swapped[0].astype(F32)
    second_sum = second_sum + swapped[1].astype(F32)
    back_got, out_got, grad_states, result = next_round(
        last, back_got, out_got, grad_states, result, [gain_chip, first_sum], [second_sum]
    )
    return (
        result[None, None],
        grad_states[None, None],
        gain_sum,
        first_sum[None],
        second_sum[None],
    )


def solution(mesh):
    return jax.shard_map(
        shards,
        mesh=mesh,
        in_specs=(
            P("section", "dp", None, None),
            P("section", None),
            P("section", "dp", "mp"),
            P("section", "dp", "mp"),
            P("dp", None),
            P("section", "dp", None, None),
        ),
        out_specs=(
            P("section", "dp", None, None),
            P("section", "dp", None, None),
            P("section", "dp"),
            P("section", "dp", "mp"),
            P("section", "dp", "mp"),
        ),
        check_vma=False,
    )
```

profile of v0, /device:TPU:6, one launch (start us, length us, event | category | flops | bytes accessed | tf_op | source)
XLA Modules:
  0.0 283.4 jit_solution(15378942001379244714)
XLA Ops:
  0.7 2.5 collective-permute-start.5
  17.8 2.7 broadcast_select_fusion.5
  26.6 2.6 fusion.38
  29.2 2.6 fusion.39
  32.8 8.5 %collective-permute-done.5 = bf16[1280,640]{1,0:T(8,128)(2,1)} collective-permute-done((bf16[1280,640]{1,0:T(8,128)(2,1)}, bf16[1280,640]{1,0:T(8,128)(2,1)}, u32[]{:S(2)}, u32[]{:S(2)}) %collective-permute-start.5) | collective-permute-done | bytes 1638432 | tf_op jit(solution)/shard_map/ppermute | solution.py:40
  48.7 32.7 %collective-permute-done.7 = bf16[1280,640]{1,0:T(8,128)(2,1)} collective-permute-done((bf16[1280,640]{1,0:T(8,128)(2,1)S(1)}, bf16[1280,640]{1,0:T(8,128)(2,1)}, u32[]{:S(2)}, u32[]{:S(2)}) %collective-permute-start.7) | collective-permute-done | bytes 1638432 | tf_op jit(solution)/shard_map/ppermute | solution.py:40
  82.1 3.2 %collective-permute-done.9 = bf16[1280,640]{1,0:T(8,128)(2,1)} collective-permute-done((bf16[1280,640]{1,0:T(8,128)(2,1)}, bf16[1280,640]{1,0:T(8,128)(2,1)}, u32[]{:S(2)}, u32[]{:S(2)}) %collective-permute-start.9) | collective-permute-done | bytes 1638432 | tf_op jit(solution)/shard_map/ppermute | solution.py:38
  88.8 4.9 %attention.1 = (bf16[256,640]{1,0:T(8,128)(2,1)S(1)}, bf16[256,640]{1,0:T(8,128)(2,1)S(1)}, bf16[2,256,640]{2,1,0:T(8,128)(2,1)S(1)}) custom-call(s32[1,2]{1,0:T(1,128)S(1)} %copy-done.2, bf16[256,640]{1,0:T(8,128)(2,1)S(1)} %copy-done.12, bf16[2,256,640]{2,1,0:T(8,128)(2,1)S(1)} %collective-permute-done.6.kv_ref, bf16[256,640]{1,0:T(8,128)(2,1)S(1)} %fusion.36.g_ref), custom_call_target="tpu_custom_call" | custom-call | flops 587202560 | bytes 2621440 | tf_op jit(solution)/shard_map/attention/pallas_call | solution.py:194
  102.9 3.5 %collective-permute-start.11 = (bf16[2,64,2560]{2,1,0:T(8,128)(2,1)S(1)}, bf16[2,64,2560]{2,1,0:T(8,128)(2,1)S(1)}, u32[]{:S(2)}, u32[]{:S(2)}) collective-permute-start(bf16[2,64,2560]{2,1,0:T(8,128)(2,1)S(1)} %fusion.41), channel_id=1, source_target_pairs={{16,17},{17,18},{18,19},{19,16},{20,21},{21,22},{22,23},{23,20},{2... | collective-permute-start | bytes 1966088 | tf_op jit(solution)/shard_map/ppermute | solution.py:40
  106.5 3.5 %collective-permute-start.10 = (bf16[2,64,2560]{2,1,0:T(8,128)(2,1)S(1)}, bf16[2,64,2560]{2,1,0:T(8,128)(2,1)S(1)}, u32[]{:S(2)}, u32[]{:S(2)}) collective-permute-start(bf16[2,64,2560]{2,1,0:T(8,128)(2,1)S(1)} %fusion.42.refs_0_), channel_id=1, source_target_pairs={{16,17},{17,18},{18,19},{19,16},{20,21},{21,22},{22,23},{23,20},{2... | collective-permute-start | bytes 1966088 | tf_op jit(solution)/shard_map/ppermute | solution.py:40
  113.0 10.8 %collective-permute-done.15 = bf16[2,256,640]{2,1,0:T(8,128)(2,1)S(1)} collective-permute-done((bf16[2,256,640]{2,1,0:T(8,128)(2,1)S(1)}, bf16[2,256,640]{2,1,0:T(8,128)(2,1)S(1)}, u32[]{:S(2)}, u32[]{:S(2)}) %collective-permute-start.15) | collective-permute-done | bytes 655392 | tf_op jit(solution)/shard_map/ppermute | solution.py:54
  127.4 3.6 %collective-permute-start.13 = (bf16[2,64,2560]{2,1,0:T(8,128)(2,1)S(1)}, bf16[2,64,2560]{2,1,0:T(8,128)(2,1)S(1)}, u32[]{:S(2)}, u32[]{:S(2)}) collective-permute-start(bf16[2,64,2560]{2,1,0:T(8,128)(2,1)S(1)} %add_block.9.refs_0_.refs_4_), channel_id=1, source_target_pairs={{16,17},{17,18},{18,19},{19,16},{20,21},{21,22},{22,23},{23,20},{2... | collective-permute-start | bytes 1966088 | tf_op jit(solution)/shard_map/ppermute | solution.py:40
  131.0 7.2 %collective-permute-done.10.got_ref = bf16[2,64,2560]{2,1,0:T(8,128)(2,1)S(1)} collective-permute-done((bf16[2,64,2560]{2,1,0:T(8,128)(2,1)S(1)}, bf16[2,64,2560]{2,1,0:T(8,128)(2,1)S(1)}, u32[]{:S(2)}, u32[]{:S(2)}) %collective-permute-start.10) | collective-permute-done | bytes 655392 | tf_op jit(solution)/shard_map/ppermute | solution.py:40
  140.8 2.9 %collective-permute-start.30 = (bf16[256,6400]{1,0:T(8,128)(2,1)S(1)}, bf16[256,6400]{1,0:T(8,128)(2,1)S(1)}, u32[]{:S(2)}, u32[]{:S(2)}) collective-permute-start(bf16[256,6400]{1,0:T(8,128)(2,1)S(1)} %join.1), channel_id=1, source_target_pairs={{16,24},{20,28},{24,16},{28,20},{17,25},{21,29},{25,17},{29,21},{1... | collective-permute-start | bytes 9830408 | tf_op jit(solution)/shard_map/ppermute | solution.py:40
  145.1 7.2 %collective-permute-done.13.got_ref = bf16[2,64,2560]{2,1,0:T(8,128)(2,1)S(1)} collective-permute-done((bf16[2,64,2560]{2,1,0:T(8,128)(2,1)S(1)}, bf16[2,64,2560]{2,1,0:T(8,128)(2,1)S(1)}, u32[]{:S(2)}, u32[]{:S(2)}) %collective-permute-start.13) | collective-permute-done | bytes 655392 | tf_op jit(solution)/shard_map/ppermute | solution.py:40
  154.6 11.8 %collective-permute-done.12.got_ref = bf16[2,64,2560]{2,1,0:T(8,128)(2,1)S(1)} collective-permute-done((bf16[2,64,2560]{2,1,0:T(8,128)(2,1)S(1)}, bf16[2,64,2560]{2,1,0:T(8,128)(2,1)S(1)}, u32[]{:S(2)}, u32[]{:S(2)}) %collective-permute-start.12) | collective-permute-done | bytes 655392 | tf_op jit(solution)/shard_map/ppermute | solution.py:40
  169.7 10.7 %collective-permute-done.20.got_ref = bf16[2,64,2560]{2,1,0:T(8,128)(2,1)S(1)} collective-permute-done((bf16[2,64,2560]{2,1,0:T(8,128)(2,1)S(1)}, bf16[2,64,2560]{2,1,0:T(8,128)(2,1)S(1)}, u32[]{:S(2)}, u32[]{:S(2)}) %collective-permute-start.20) | collective-permute-done | bytes 655392 | tf_op jit(solution)/shard_map/ppermute | solution.py:40
  190.2 4.3 %collective-permute-done.14.got_ref = bf16[2,64,2560]{2,1,0:T(8,128)(2,1)S(1)} collective-permute-done((bf16[2,64,2560]{2,1,0:T(8,128)(2,1)S(1)}, bf16[2,64,2560]{2,1,0:T(8,128)(2,1)S(1)}, u32[]{:S(2)}, u32[]{:S(2)}) %collective-permute-start.14) | collective-permute-done | bytes 655392 | tf_op jit(solution)/shard_map/ppermute | solution.py:40
  195.2 3.7 %collective-permute-start.22 = (bf16[64,5120]{1,0:T(8,128)(2,1)S(1)}, bf16[64,5120]{1,0:T(8,128)(2,1)S(1)}, u32[]{:S(2)}, u32[]{:S(2)}) collective-permute-start(bf16[64,5120]{1,0:T(8,128)(2,1)S(1)} %fusion.24.refs_0_.rows_ref), channel_id=1, source_target_pairs={{16,17},{17,18},{18,19},{19,16},{20,21},{21,22},{22,23},{23,20},{2... | collective-permute-start | bytes 1966088 | tf_op jit(solution)/shard_map/ppermute | solution.py:40
  199.0 14.9 %collective-permute-done.25.rows_ref.other_ref = bf16[64,5120]{1,0:T(8,128)(2,1)S(1)} collective-permute-done((bf16[64,5120]{1,0:T(8,128)(2,1)S(1)}, bf16[64,5120]{1,0:T(8,128)(2,1)S(1)}, u32[]{:S(2)}, u32[]{:S(2)}) %collective-permute-start.25) | collective-permute-done | bytes 655392 | tf_op jit(solution)/shard_map/ppermute | solution.py:38
  215.5 12.5 %collective-permute-done.22.rows_ref = bf16[64,5120]{1,0:T(8,128)(2,1)S(1)} collective-permute-done((bf16[64,5120]{1,0:T(8,128)(2,1)S(1)}, bf16[64,5120]{1,0:T(8,128)(2,1)S(1)}, u32[]{:S(2)}, u32[]{:S(2)}) %collective-permute-start.22) | collective-permute-done | bytes 655392 | tf_op jit(solution)/shard_map/ppermute | solution.py:40
  246.4 9.6 %collective-permute-done.23.rows_ref = bf16[64,5120]{1,0:T(8,128)(2,1)S(1)} collective-permute-done((bf16[64,5120]{1,0:T(8,128)(2,1)S(1)}, bf16[64,5120]{1,0:T(8,128)(2,1)S(1)}, u32[]{:S(2)}, u32[]{:S(2)}) %collective-permute-start.23) | collective-permute-done | bytes 655392 | tf_op jit(solution)/shard_map/ppermute | solution.py:40
  264.8 5.3 %collective-permute-done.31.rows_ref.other_ref = bf16[64,5120]{1,0:T(8,128)(2,1)S(1)} collective-permute-done((bf16[64,5120]{1,0:T(8,128)(2,1)S(1)}, bf16[64,5120]{1,0:T(8,128)(2,1)S(1)}, u32[]{:S(2)}, u32[]{:S(2)}) %collective-permute-start.31) | collective-permute-done | bytes 655392 | tf_op jit(solution)/shard_map/ppermute | solution.py:38
  272.9 8.9 %collective-permute-done.24.rows_ref = bf16[64,5120]{1,0:T(8,128)(2,1)S(1)} collective-permute-done((bf16[64,5120]{1,0:T(8,128)(2,1)S(1)}, bf16[64,5120]{1,0:T(8,128)(2,1)S(1)}, u32[]{:S(2)}, u32[]{:S(2)}) %collective-permute-start.24) | collective-permute-done | bytes 655392 | tf_op jit(solution)/shard_map/ppermute | solution.py:40
  (226 shorter events, 101.4 us)
Async XLA Ops:
  0.6 21.1 %collective-permute-start.1 = (bf16[1280,640]{1,0:T(8,128)(2,1)}, bf16[1280,640]{1,0:T(8,128)(2,1)}, u32[]{:S(2)}, u32[]{:S(2)}) collective-permute-start(bf16[1280,640]{1,0:T(8,128)(2,1)} %bitcast.127), channel_id=1, source_target_pairs={{0,4},{4,0},{8,12},{12,8},{1,5},{5,1},{9,13},{13,9},{2,6},{6,2},{1... | collective-permute-start | bytes 4915208 | tf_op jit(solution)/shard_map/ppermute | solution.py:38
  0.7 40.5 %collective-permute-start.5 = (bf16[1280,640]{1,0:T(8,128)(2,1)}, bf16[1280,640]{1,0:T(8,128)(2,1)}, u32[]{:S(2)}, u32[]{:S(2)}) collective-permute-start(bf16[1280,640]{1,0:T(8,128)(2,1)} %bitcast.128), channel_id=1, source_target_pairs={{16,24},{20,28},{24,16},{28,20},{17,25},{21,29},{25,17},{29,21},{1... | collective-permute-start | bytes 4915208 | tf_op jit(solution)/shard_map/ppermute | solution.py:40
  6.0 20.1 %collective-permute-start = (bf16[256,2560]{1,0:T(8,128)(2,1)}, bf16[256,2560]{1,0:T(8,128)(2,1)}, u32[]{:S(2)}, u32[]{:S(2)}) collective-permute-start(bf16[256,2560]{1,0:T(8,128)(2,1)} %dynamic-slice_bitcast_fusion), channel_id=1, source_target_pairs={{0,8},{4,12},{8,0},{12,4},{1,9},{5,13},{9,1},{13,5},{2,10},{6,14},... | collective-permute-start | bytes 3932168 | tf_op jit(solution)/shard_map/ppermute | solution.py:40
  8.5 17.6 %collective-permute-start.3 = (f32[1,256]{1,0:T(1,128)S(1)}, f32[1,256]{1,0:T(1,128)S(1)}, u32[]{:S(2)}, u32[]{:S(2)}) collective-permute-start(f32[1,256]{1,0:T(1,128)S(1)} %bitcast.140), channel_id=1, source_target_pairs={{0,8},{4,12},{8,0},{12,4},{1,9},{5,13},{9,1},{13,5},{2,10},{6,14},... | collective-permute-start | bytes 3080 | tf_op jit(solution)/shard_map/ppermute | solution.py:40
  41.3 40.2 %collective-permute-start.7 = (bf16[1280,640]{1,0:T(8,128)(2,1)S(1)}, bf16[1280,640]{1,0:T(8,128)(2,1)}, u32[]{:S(2)}, u32[]{:S(2)}) collective-permute-start(bf16[1280,640]{1,0:T(8,128)(2,1)S(1)} %bitcast.130), channel_id=1, source_target_pairs={{16,24},{20,28},{24,16},{28,20},{17,25},{21,29},{25,17},{29,21},{1... | collective-permute-start | bytes 4915208 | tf_op jit(solution)/shard_map/ppermute | solution.py:40
  43.7 37.8 %collective-permute-start.6 = (bf16[2,256,640]{2,1,0:T(8,128)(2,1)S(1)}, bf16[2,256,640]{2,1,0:T(8,128)(2,1)S(1)}, u32[]{:S(2)}, u32[]{:S(2)}) collective-permute-start(bf16[2,256,640]{2,1,0:T(8,128)(2,1)S(1)} %fusion.33), channel_id=1, source_target_pairs={{0,16},{1,17},{2,18},{3,19},{4,20},{5,21},{6,22},{7,23},{8,24},{9,... | collective-permute-start | bytes 1966088 | tf_op jit(solution)/shard_map/ppermute | solution.py:277
  93.7 16.8 %collective-permute-start.16 = (bf16[2,256,640]{2,1,0:T(8,128)(2,1)S(1)}, bf16[2,256,640]{2,1,0:T(8,128)(2,1)S(1)}, u32[]{:S(2)}, u32[]{:S(2)}) collective-permute-start(bf16[2,256,640]{2,1,0:T(8,128)(2,1)S(1)} %get-tuple-element.30), channel_id=1, source_target_pairs={{16,8},{20,12},{24,0},{28,4},{17,9},{21,13},{25,1},{29,5},{18,10},... | collective-permute-start | bytes 1966088 | tf_op jit(solution)/shard_map/ppermute | solution.py:54
  95.2 28.6 %collective-permute-start.15 = (bf16[2,256,640]{2,1,0:T(8,128)(2,1)S(1)}, bf16[2,256,640]{2,1,0:T(8,128)(2,1)S(1)}, u32[]{:S(2)}, u32[]{:S(2)}) collective-permute-start(bf16[2,256,640]{2,1,0:T(8,128)(2,1)S(1)} %get-tuple-element.30), channel_id=1, source_target_pairs={{16,0},{20,4},{24,8},{28,12},{17,1},{21,5},{25,9},{29,13},{18,2},{... | collective-permute-start | bytes 1966088 | tf_op jit(solution)/shard_map/ppermute | solution.py:54
  102.9 24.1 %collective-permute-start.11 = (bf16[2,64,2560]{2,1,0:T(8,128)(2,1)S(1)}, bf16[2,64,2560]{2,1,0:T(8,128)(2,1)S(1)}, u32[]{:S(2)}, u32[]{:S(2)}) collective-permute-start(bf16[2,64,2560]{2,1,0:T(8,128)(2,1)S(1)} %fusion.41), channel_id=1, source_target_pairs={{16,17},{17,18},{18,19},{19,16},{20,21},{21,22},{22,23},{23,20},{2... | collective-permute-start | bytes 1966088 | tf_op jit(solution)/shard_map/ppermute | solution.py:40
  106.5 31.8 %collective-permute-start.10 = (bf16[2,64,2560]{2,1,0:T(8,128)(2,1)S(1)}, bf16[2,64,2560]{2,1,0:T(8,128)(2,1)S(1)}, u32[]{:S(2)}, u32[]{:S(2)}) collective-permute-start(bf16[2,64,2560]{2,1,0:T(8,128)(2,1)S(1)} %fusion.42.refs_0_), channel_id=1, source_target_pairs={{16,17},{17,18},{18,19},{19,16},{20,21},{21,22},{22,23},{23,20},{2... | collective-permute-start | bytes 1966088 | tf_op jit(solution)/shard_map/ppermute | solution.py:40
  126.3 17.8 %collective-permute-start.17 = (bf16[2,64,2560]{2,1,0:T(8,128)(2,1)S(1)}, bf16[2,64,2560]{2,1,0:T(8,128)(2,1)S(1)}, u32[]{:S(2)}, u32[]{:S(2)}) collective-permute-start(bf16[2,64,2560]{2,1,0:T(8,128)(2,1)S(1)} %fusion.40), channel_id=1, source_target_pairs={{0,1},{1,2},{2,3},{3,0},{4,5},{5,6},{6,7},{7,4},{8,9},{9,10},{10,1... | collective-permute-start | bytes 1966088 | tf_op jit(solution)/shard_map/ppermute | solution.py:40
  127.4 24.9 %collective-permute-start.13 = (bf16[2,64,2560]{2,1,0:T(8,128)(2,1)S(1)}, bf16[2,64,2560]{2,1,0:T(8,128)(2,1)S(1)}, u32[]{:S(2)}, u32[]{:S(2)}) collective-permute-start(bf16[2,64,2560]{2,1,0:T(8,128)(2,1)S(1)} %add_block.9.refs_0_.refs_4_), channel_id=1, source_target_pairs={{16,17},{17,18},{18,19},{19,16},{20,21},{21,22},{22,23},{23,20},{2... | collective-permute-start | bytes 1966088 | tf_op jit(solution)/shard_map/ppermute | solution.py:40
  138.6 27.7 %collective-permute-start.12 = (bf16[2,64,2560]{2,1,0:T(8,128)(2,1)S(1)}, bf16[2,64,2560]{2,1,0:T(8,128)(2,1)S(1)}, u32[]{:S(2)}, u32[]{:S(2)}) collective-permute-start(bf16[2,64,2560]{2,1,0:T(8,128)(2,1)S(1)} %add_block.10.refs_0_), channel_id=1, source_target_pairs={{16,17},{17,18},{18,19},{19,16},{20,21},{21,22},{22,23},{23,20},{2... | collective-permute-start | bytes 1966088 | tf_op jit(solution)/shard_map/ppermute | solution.py:40
  140.8 98.9 %collective-permute-start.30 = (bf16[256,6400]{1,0:T(8,128)(2,1)S(1)}, bf16[256,6400]{1,0:T(8,128)(2,1)S(1)}, u32[]{:S(2)}, u32[]{:S(2)}) collective-permute-start(bf16[256,6400]{1,0:T(8,128)(2,1)S(1)} %join.1), channel_id=1, source_target_pairs={{16,24},{20,28},{24,16},{28,20},{17,25},{21,29},{25,17},{29,21},{1... | collective-permute-start | bytes 9830408 | tf_op jit(solution)/shard_map/ppermute | solution.py:40
  144.4 24.2 %collective-permute-start.18 = (bf16[2,64,2560]{2,1,0:T(8,128)(2,1)S(1)}, bf16[2,64,2560]{2,1,0:T(8,128)(2,1)S(1)}, u32[]{:S(2)}, u32[]{:S(2)}) collective-permute-start(bf16[2,64,2560]{2,1,0:T(8,128)(2,1)S(1)} %add_block.13), channel_id=1, source_target_pairs={{0,1},{1,2},{2,3},{3,0},{4,5},{5,6},{6,7},{7,4},{8,9},{9,10},{10,1... | collective-permute-start | bytes 1966088 | tf_op jit(solution)/shard_map/ppermute | solution.py:40
  152.6 27.7 %collective-permute-start.20 = (bf16[2,64,2560]{2,1,0:T(8,128)(2,1)S(1)}, bf16[2,64,2560]{2,1,0:T(8,128)(2,1)S(1)}, u32[]{:S(2)}, u32[]{:S(2)}) collective-permute-start(bf16[2,64,2560]{2,1,0:T(8,128)(2,1)S(1)} %add_block.11.refs_0_), channel_id=1, source_target_pairs={{16,17},{17,18},{18,19},{19,16},{20,21},{21,22},{22,23},{23,20},{2... | collective-permute-start | bytes 1966088 | tf_op jit(solution)/shard_map/ppermute | solution.py:40
  166.7 27.8 %collective-permute-start.14 = (bf16[2,64,2560]{2,1,0:T(8,128)(2,1)S(1)}, bf16[2,64,2560]{2,1,0:T(8,128)(2,1)S(1)}, u32[]{:S(2)}, u32[]{:S(2)}) collective-permute-start(bf16[2,64,2560]{2,1,0:T(8,128)(2,1)S(1)} %add_block.12.refs_0_), channel_id=1, source_target_pairs={{16,17},{17,18},{18,19},{19,16},{20,21},{21,22},{22,23},{23,20},{2... | collective-permute-start | bytes 1966088 | tf_op jit(solution)/shard_map/ppermute | solution.py:40
  194.5 19.5 %collective-permute-start.25 = (bf16[64,5120]{1,0:T(8,128)(2,1)S(1)}, bf16[64,5120]{1,0:T(8,128)(2,1)S(1)}, u32[]{:S(2)}, u32[]{:S(2)}) collective-permute-start(bf16[64,5120]{1,0:T(8,128)(2,1)S(1)} %fusion.22.refs_0_.rows_ref.other_ref), channel_id=1, source_target_pairs={{0,1},{1,2},{2,3},{3,0},{4,5},{5,6},{6,7},{7,4},{8,9},{9,10},{10,1... | collective-permute-start | bytes 1966088 | tf_op jit(solution)/shard_map/ppermute | solution.py:38
  195.2 32.8 %collective-permute-start.22 = (bf16[64,5120]{1,0:T(8,128)(2,1)S(1)}, bf16[64,5120]{1,0:T(8,128)(2,1)S(1)}, u32[]{:S(2)}, u32[]{:S(2)}) collective-permute-start(bf16[64,5120]{1,0:T(8,128)(2,1)S(1)} %fusion.24.refs_0_.rows_ref), channel_id=1, source_target_pairs={{16,17},{17,18},{18,19},{19,16},{20,21},{21,22},{22,23},{23,20},{2... | collective-permute-start | bytes 1966088 | tf_op jit(solution)/shard_map/ppermute | solution.py:40
  214.0 31.7 %collective-permute-start.26 = (bf16[64,5120]{1,0:T(8,128)(2,1)S(1)}, bf16[64,5120]{1,0:T(8,128)(2,1)S(1)}, u32[]{:S(2)}, u32[]{:S(2)}) collective-permute-start(bf16[64,5120]{1,0:T(8,128)(2,1)S(1)} %collective-permute-done.25.rows_ref.other_ref), channel_id=1, source_target_pairs={{0,1},{1,2},{2,3},{3,0},{4,5},{5,6},{6,7},{7,4},{8,9},{9,10},{10,1... | collective-permute-start | bytes 1966088 | tf_op jit(solution)/shard_map/ppermute | solution.py:38
  228.0 28.1 %collective-permute-start.23 = (bf16[64,5120]{1,0:T(8,128)(2,1)S(1)}, bf16[64,5120]{1,0:T(8,128)(2,1)S(1)}, u32[]{:S(2)}, u32[]{:S(2)}) collective-permute-start(bf16[64,5120]{1,0:T(8,128)(2,1)S(1)} %collective-permute-done.22.rows_ref), channel_id=1, source_target_pairs={{16,17},{17,18},{18,19},{19,16},{20,21},{21,22},{22,23},{23,20},{2... | collective-permute-start | bytes 1966088 | tf_op jit(solution)/shard_map/ppermute | solution.py:40
  245.6 17.9 %collective-permute-start.33 = (bf16[2,1280,640]{2,1,0:T(8,128)(2,1)S(1)}, bf16[2,1280,640]{2,1,0:T(8,128)(2,1)S(1)}, u32[]{:S(2)}, u32[]{:S(2)}) collective-permute-start(bf16[2,1280,640]{2,1,0:T(8,128)(2,1)S(1)} %pad_maximum_fusion.4.refs_2_), channel_id=1, source_target_pairs={{0,4},{4,0},{8,12},{12,8},{1,5},{5,1},{9,13},{13,9},{2,6},{6,2},{1... | collective-permute-start | bytes 9830408 | tf_op jit(solution)/shard_map/ppermute | solution.py:38
  246.4 23.7 %collective-permute-start.31 = (bf16[64,5120]{1,0:T(8,128)(2,1)S(1)}, bf16[64,5120]{1,0:T(8,128)(2,1)S(1)}, u32[]{:S(2)}, u32[]{:S(2)}) collective-permute-start(bf16[64,5120]{1,0:T(8,128)(2,1)S(1)} %collective-permute-done.26.refs_0_.rows_ref.other_ref), channel_id=1, source_target_pairs={{0,1},{1,2},{2,3},{3,0},{4,5},{5,6},{6,7},{7,4},{8,9},{9,10},{10,1... | collective-permute-start | bytes 1966088 | tf_op jit(solution)/shard_map/ppermute | solution.py:38
  256.1 25.7 %collective-permute-start.24 = (bf16[64,5120]{1,0:T(8,128)(2,1)S(1)}, bf16[64,5120]{1,0:T(8,128)(2,1)S(1)}, u32[]{:S(2)}, u32[]{:S(2)}) collective-permute-start(bf16[64,5120]{1,0:T(8,128)(2,1)S(1)} %collective-permute-done.23.rows_ref), channel_id=1, source_target_pairs={{16,17},{17,18},{18,19},{19,16},{20,21},{21,22},{22,23},{23,20},{2... | collective-permute-start | bytes 1966088 | tf_op jit(solution)/shard_map/ppermute | solution.py:40
  (57 other events, 303.2 us)
where the time goes:
time: 285 us; the launch traced here: 283 us
  waiting for transfers between devices  148 us (52%)
  starting transfers between devices  47.3 us (17%)
  matrix products  25.3 us (9%)
  other arithmetic  24.1 us (8%)
  Pallas kernels  20.8 us (7%)
  local copies, waits for them, and re-layouts  16.4 us (6%)
    ppermute x19, waiting for transfers between devices, permute(): return lax.ppermute(x, ('section', axis), pairs)  113 us
    ppermute x19, starting transfers between devices, permute(): return lax.ppermute(x, ('section', axis), pairs)  38.1 us
    ppermute x13, waiting for transfers between devices, permute(): return lax.ppermute(x, axis, [(i, to(i, n)) for i in range(n)])  23.4 us
    unnamed x92, local copies, waits for them, and re-layouts  12.9 us
    pallas_call x8, Pallas kernels, place_block(): pl.pallas_call(place_kernel, grid_spec=pltpu.PrefetchScalarGridSpec(num_s...  12.3 us
    ppermute x2, waiting for transfers between devices, home_shift(): return lax.ppermute(x, ('section', 'dp'), pairs)  10.8 us
    dot_general x6, matrix products, dot_plain(): return jnp.dot(left, right, preferred_element_type=F32)  10.6 us
    dot_general x8, matrix products, dot_last(): lax.dot_general(left, right, (((1,), (1,)), ((), ())), preferred_element_...  9.71 us
  transfers between devices with their start and end apart: 35, of which 14 were waited for; matrix products, arithmetic and copies ran while one was open for 17% of the time, Pallas kernels for 5%

commit v1 on v0

--- a/solution.py
+++ b/solution.py
@@ -90,30 +90,41 @@
 
 
 def place_kernel(place_ref, rows_ref, other_ref, *refs):
-    refs[-1][...] = jnp.where(place_ref[1] == 1, rows_ref[...], other_ref[...])
+    out_ref, token_ref, ready, sem = refs[-4:]
+    token_ref[...] = jnp.zeros_like(token_ref)
+    tokens = rows_ref.shape[0]
+    at = pl.multiple_of(place_ref[0] * tokens, tokens)
+    ready[...] = jnp.where(place_ref[1] == 1, rows_ref[...], other_ref[...])
+    copy = pltpu.make_async_copy(ready, out_ref.at[pl.ds(at, tokens)], sem)
+    copy.start()
+    copy.wait()
 
 
 def place_block(whole, length, rows, place, other, wanted, *before):
     tokens, features = rows.shape
-    steps = 2 if features % 256 == 0 else 1
-    piece = features // steps
     where = jnp.stack([place, wanted.astype(jnp.int32)])
-    block = pl.BlockSpec((tokens, piece), lambda i, at: (at[0], i))
-    mine = pl.BlockSpec((tokens, piece), lambda i, at: (0, i))
+    mine = pl.BlockSpec((tokens, features), lambda i, at: (0, 0))
     whole = [] if whole is None else [whole]
     if other is None:
         other, other_block = rows, mine
     else:
-        other_block = block
+        other_block = pl.BlockSpec((tokens, features), lambda i, at: (at[0], 0))
     return pl.pallas_call(
         place_kernel,
         grid_spec=pltpu.PrefetchScalarGridSpec(
             num_scalar_prefetch=1,
-            grid=(steps,),
+            grid=(1,),
             in_specs=[mine, other_block] + [ANYWHERE] * len(whole + list(before)),
-            out_specs=block,
+            out_specs=[ANYWHERE, pl.BlockSpec((8, 128), lambda i, at: (0, 0))],
+            scratch_shapes=[
+                pltpu.VMEM((tokens, features), rows.dtype),
+                pltpu.SemaphoreType.DMA,
+            ],
         ),
-        out_shape=jax.ShapeDtypeStruct((length, features), rows.dtype),
+        out_shape=[
+            jax.ShapeDtypeStruct((length, features), rows.dtype),
+            jax.ShapeDtypeStruct((8, 128), F32),
+        ],
         input_output_aliases={3: 0} if whole else {},
         compiler_params=pltpu.CompilerParams(vmem_limit_bytes=32 * 2**20),
         cost_estimate=pl.CostEstimate(flops=WAIT, bytes_accessed=0, transcendentals=0),
@@ -289,8 +300,6 @@
         grad_context = grad_context + dot_plain(grad_columns[k - 1], second_far[k - 1])
     grad_context = grad_context.astype(BF16)
     context, grad_query, grad_memory = attention(lengths, queries, memory_heads, grad_context)
-    grad_memory, *far_memory = [home_shift(grad_memory, k) for k in range(chips)]
-
     def block_at(array, place):
         at = lax.rem(place + 2 * heads_axis, heads_axis) * block
         return lax.dynamic_slice_in_dim(array, at, block, array.ndim - 2)
@@ -330,6 +339,10 @@
     out_parts = piled(dot_last(context, w) for w in [second_chip] + second_far)
     out_held = first_block(out_parts)
     out_got = send_out(out_held)
+    leaving = pass_on(grad_memory.reshape(2 * length, columns), back_held)
+    leaving = leaving.reshape(2, length, columns)
+    grad_memory, *far_memory = [home_shift(leaving, k) for k in range(chips)]
+
     memory_parts = piled(
         dot_last(g[0], first_chip) + dot_last(g[1], second_chip)
         for g in [grad_memory] + far_memory
@@ -387,25 +400,25 @@
     def place_out(whole, rows, step, *before):
         return place_block(whole, length, rows, at(step), normed, decoder, *before)
 
-    def next_round(step, back_got, out_got, grad_states, result, first, then):
+    def next_round(step, back_got, out_got, grad_states, result, token, first, then):
         arrived = back_got
         if step < last:
             back_got = head_shift(arrived, 1)
-        grad_states = place_grad(grad_states, arrived, step, result, *first)
+        grad_states, token = place_grad(grad_states, arrived, step, token, *first)
         arrived = out_got
         if step < last:
             out_got = send_out(arrived)
-        result = place_out(result, arrived, step, grad_states, *then)
-        return back_got, out_got, grad_states, result
+        result, token = place_out(result, arrived, step, token, *then)
+        return back_got, out_got, grad_states, result, token
 
     arrived = back_got
     back_got = head_shift(arrived, 1)
-    grad_states = place_grad(None, arrived, 1, out_held)
+    grad_states, token = place_grad(None, arrived, 1, out_held)
     arrived = out_got
     out_got = send_out(arrived)
-    result = place_out(None, arrived, 1, grad_states)
-    grad_states = place_grad(grad_states, back_held, 0, result)
-    result = place_out(result, out_held, 0, grad_states)
+    result, token = place_out(None, arrived, 1, token)
+    grad_states, token = place_grad(grad_states, back_held, 0, token)
+    result, token = place_out(result, out_held, 0, token)
     for part in gain_parts:
         gain_part = gain_part + part
     gain_part = pass_on(gain_part, back_got)
@@ -431,8 +444,8 @@
     halves = jnp.stack([x.astype(BF16) for x in weight_grads(1 - core)])
     swapped = core_swap(halves)
     for step in range(2, last):
-        back_got, out_got, grad_states, result = next_round(
-            step, back_got, out_got, grad_states, result, [gain_part], [halves]
+        back_got, out_got, grad_states, result, token = next_round(
+            step, back_got, out_got, grad_states, result, token, [gain_part], [halves]
         )
     for part in gain_far:
         gain_chip = gain_chip + part
@@ -443,8 +456,8 @@
     first_sum, second_sum = weight_grads(core)
     first_sum = first_sum + swapped[0].astype(F32)
     second_sum = second_sum + swapped[1].astype(F32)
-    back_got, out_got, grad_states, result = next_round(
-        last, back_got, out_got, grad_states, result, [gain_chip, first_sum], [second_sum]
+    back_got, out_got, grad_states, result, token = next_round(
+        last, back_got, out_got, grad_states, result, token, [gain_chip, first_sum], [second_sum]
     )
     return (
         result[None, None],

time: 285 us -> 284 us (level)
  local copies, waits for them, and re-layouts: 16.4 us -> 9.5 us
  waiting for transfers between devices: 148 us -> 152 us
    unnamed x92 -> x78, local copies, waits for them, and re-layouts: 12.9 us -> 6.02 us
    ppermute x13, waiting for transfers between devices: 23.4 us -> 26.9 us  [permute(): return lax.ppermute(x, axis, [(i, to(i, n)) for i in range(n)])]
    ppermute x2, waiting for transfers between devices: 10.8 us -> 14.1 us  [home_shift(): return lax.ppermute(x, ('section', 'dp'), pairs)]
  transfers between devices with their start and end apart: 35 -> 35, of which waited for: 14 -> 15; matrix products, arithmetic and copies ran while one was open for 17% -> 17% of each run, Pallas kernels for 5% -> 5%
where the time goes in v1:
time: 284 us; the launch traced here: 283 us
  waiting for transfers between devices  152 us (54%)
  starting transfers between devices  48.7 us (17%)
  matrix products  25.3 us (9%)
  other arithmetic  24.1 us (8%)
  Pallas kernels  20.7 us (7%)
  local copies, waits for them, and re-layouts  9.5 us (3%)
    ppermute x19, waiting for transfers between devices, permute(): return lax.ppermute(x, ('section', axis), pairs)  111 us
    ppermute x19, starting transfers between devices, permute(): return lax.ppermute(x, ('section', axis), pairs)  39.8 us
    ppermute x13, waiting for transfers between devices, permute(): return lax.ppermute(x, axis, [(i, to(i, n)) for i in range(n)])  26.9 us
    ppermute x2, waiting for transfers between devices, home_shift(): return lax.ppermute(x, ('section', 'dp'), pairs)  14.1 us
    pallas_call x8, Pallas kernels, place_block(): pl.pallas_call(place_kernel, grid_spec=pltpu.PrefetchScalarGridSpec(num_s...  12.2 us
    dot_general x6, matrix products, dot_plain(): return jnp.dot(left, right, preferred_element_type=F32)  10.6 us
    dot_general x8, matrix products, dot_last(): lax.dot_general(left, right, (((1,), (1,)), ((), ())), preferred_element_...  9.69 us
    select_n x4, other arithmetic, in_order(): ahead = [jnp.where(core == 0, a, b) for a, b in zip(own, other)]  8.41 us
  transfers between devices with their start and end apart: 35, of which 15 were waited for; matrix products, arithmetic and copies ran while one was open for 17% of the time, Pallas kernels for 5%

profile of v1, /device:TPU:6, one launch (start us, length us, event | category | flops | bytes accessed | tf_op | source)
XLA Modules:
  0.0 282.6 jit_solution(8543197222236029221)
XLA Ops:
  17.8 2.7 broadcast_select_fusion.5
  26.6 2.6 fusion.38
  29.2 2.6 fusion.39
  32.8 8.5 %collective-permute-done.5 = bf16[1280,640]{1,0:T(8,128)(2,1)} collective-permute-done((bf16[1280,640]{1,0:T(8,128)(2,1)}, bf16[1280,640]{1,0:T(8,128)(2,1)}, u32[]{:S(2)}, u32[]{:S(2)}) %collective-permute-start.5) | collective-permute-done | bytes 1638432 | tf_op jit(solution)/shard_map/ppermute | solution.py:40
  48.9 32.6 %collective-permute-done.7 = bf16[1280,640]{1,0:T(8,128)(2,1)} collective-permute-done((bf16[1280,640]{1,0:T(8,128)(2,1)S(1)}, bf16[1280,640]{1,0:T(8,128)(2,1)}, u32[]{:S(2)}, u32[]{:S(2)}) %collective-permute-start.7) | collective-permute-done | bytes 1638432 | tf_op jit(solution)/shard_map/ppermute | solution.py:40
  82.1 3.2 %collective-permute-done.9 = bf16[1280,640]{1,0:T(8,128)(2,1)} collective-permute-done((bf16[1280,640]{1,0:T(8,128)(2,1)}, bf16[1280,640]{1,0:T(8,128)(2,1)}, u32[]{:S(2)}, u32[]{:S(2)}) %collective-permute-start.9) | collective-permute-done | bytes 1638432 | tf_op jit(solution)/shard_map/ppermute | solution.py:38
  88.8 4.9 %attention.1 = (bf16[256,640]{1,0:T(8,128)(2,1)S(1)}, bf16[256,640]{1,0:T(8,128)(2,1)S(1)}, bf16[2,256,640]{2,1,0:T(8,128)(2,1)S(1)}) custom-call(s32[1,2]{1,0:T(1,128)S(1)} %copy-done.2, bf16[256,640]{1,0:T(8,128)(2,1)S(1)} %copy-done.5, bf16[2,256,640]{2,1,0:T(8,128)(2,1)S(1)} %collective-permute-done.6.kv_ref, bf16[256,640]{1,0:T(8,128)(2,1)S(1)} %fusion.36.g_ref), custom_call_target="tpu_custom_call" | custom-call | flops 587202560 | bytes 2621440 | tf_op jit(solution)/shard_map/attention/pallas_call | solution.py:205
  99.7 3.5 %collective-permute-start.11 = (bf16[2,64,2560]{2,1,0:T(8,128)(2,1)S(1)}, bf16[2,64,2560]{2,1,0:T(8,128)(2,1)S(1)}, u32[]{:S(2)}, u32[]{:S(2)}) collective-permute-start(bf16[2,64,2560]{2,1,0:T(8,128)(2,1)S(1)} %fusion.41.refs_0_), channel_id=1, source_target_pairs={{16,17},{17,18},{18,19},{19,16},{20,21},{21,22},{22,23},{23,20},{2... | collective-permute-start | bytes 1966088 | tf_op jit(solution)/shard_map/ppermute | solution.py:40
  106.4 3.5 %collective-permute-start.10 = (bf16[2,64,2560]{2,1,0:T(8,128)(2,1)S(1)}, bf16[2,64,2560]{2,1,0:T(8,128)(2,1)S(1)}, u32[]{:S(2)}, u32[]{:S(2)}) collective-permute-start(bf16[2,64,2560]{2,1,0:T(8,128)(2,1)S(1)} %fusion.42.refs_0_), channel_id=1, source_target_pairs={{16,17},{17,18},{18,19},{19,16},{20,21},{21,22},{22,23},{23,20},{2... | collective-permute-start | bytes 1966088 | tf_op jit(solution)/shard_map/ppermute | solution.py:40
  110.4 3.0 %collective-permute-done.16 = bf16[2,256,640]{2,1,0:T(8,128)(2,1)S(1)} collective-permute-done((bf16[2,256,640]{2,1,0:T(8,128)(2,1)S(1)}, bf16[2,256,640]{2,1,0:T(8,128)(2,1)S(1)}, u32[]{:S(2)}, u32[]{:S(2)}) %collective-permute-start.16) | collective-permute-done | bytes 655392 | tf_op jit(solution)/shard_map/ppermute | solution.py:54
  115.8 11.1 %collective-permute-done.15 = bf16[2,256,640]{2,1,0:T(8,128)(2,1)S(1)} collective-permute-done((bf16[2,256,640]{2,1,0:T(8,128)(2,1)S(1)}, bf16[2,256,640]{2,1,0:T(8,128)(2,1)S(1)}, u32[]{:S(2)}, u32[]{:S(2)}) %collective-permute-start.15) | collective-permute-done | bytes 655392 | tf_op jit(solution)/shard_map/ppermute | solution.py:54
  130.5 3.8 %collective-permute-start.13 = (bf16[2,64,2560]{2,1,0:T(8,128)(2,1)S(1)}, bf16[2,64,2560]{2,1,0:T(8,128)(2,1)S(1)}, u32[]{:S(2)}, u32[]{:S(2)}) collective-permute-start(bf16[2,64,2560]{2,1,0:T(8,128)(2,1)S(1)} %add_block.9.refs_0_.refs_4_), channel_id=1, source_target_pairs={{16,17},{17,18},{18,19},{19,16},{20,21},{21,22},{22,23},{23,20},{2... | collective-permute-start | bytes 1966088 | tf_op jit(solution)/shard_map/ppermute | solution.py:40
  134.7 3.5 %collective-permute-start.12 = (bf16[2,64,2560]{2,1,0:T(8,128)(2,1)S(1)}, bf16[2,64,2560]{2,1,0:T(8,128)(2,1)S(1)}, u32[]{:S(2)}, u32[]{:S(2)}) collective-permute-start(bf16[2,64,2560]{2,1,0:T(8,128)(2,1)S(1)} %add_block.10.refs_0_), channel_id=1, source_target_pairs={{16,17},{17,18},{18,19},{19,16},{20,21},{21,22},{22,23},{23,20},{2... | collective-permute-start | bytes 1966088 | tf_op jit(solution)/shard_map/ppermute | solution.py:40
  138.5 2.7 collective-permute-start.30
  142.7 9.3 %collective-permute-done.13.got_ref = bf16[2,64,2560]{2,1,0:T(8,128)(2,1)S(1)} collective-permute-done((bf16[2,64,2560]{2,1,0:T(8,128)(2,1)S(1)}, bf16[2,64,2560]{2,1,0:T(8,128)(2,1)S(1)}, u32[]{:S(2)}, u32[]{:S(2)}) %collective-permute-start.13) | collective-permute-done | bytes 655392 | tf_op jit(solution)/shard_map/ppermute | solution.py:40
  154.2 11.8 %collective-permute-done.12.got_ref = bf16[2,64,2560]{2,1,0:T(8,128)(2,1)S(1)} collective-permute-done((bf16[2,64,2560]{2,1,0:T(8,128)(2,1)S(1)}, bf16[2,64,2560]{2,1,0:T(8,128)(2,1)S(1)}, u32[]{:S(2)}, u32[]{:S(2)}) %collective-permute-start.12) | collective-permute-done | bytes 655392 | tf_op jit(solution)/shard_map/ppermute | solution.py:40
  169.4 10.7 %collective-permute-done.20.got_ref = bf16[2,64,2560]{2,1,0:T(8,128)(2,1)S(1)} collective-permute-done((bf16[2,64,2560]{2,1,0:T(8,128)(2,1)S(1)}, bf16[2,64,2560]{2,1,0:T(8,128)(2,1)S(1)}, u32[]{:S(2)}, u32[]{:S(2)}) %collective-permute-start.20) | collective-permute-done | bytes 655392 | tf_op jit(solution)/shard_map/ppermute | solution.py:40
  189.7 3.8 %collective-permute-done.14.got_ref = bf16[2,64,2560]{2,1,0:T(8,128)(2,1)S(1)} collective-permute-done((bf16[2,64,2560]{2,1,0:T(8,128)(2,1)S(1)}, bf16[2,64,2560]{2,1,0:T(8,128)(2,1)S(1)}, u32[]{:S(2)}, u32[]{:S(2)}) %collective-permute-start.14) | collective-permute-done | bytes 655392 | tf_op jit(solution)/shard_map/ppermute | solution.py:40
  194.3 3.7 %collective-permute-start.22 = (bf16[64,5120]{1,0:T(8,128)(2,1)S(1)}, bf16[64,5120]{1,0:T(8,128)(2,1)S(1)}, u32[]{:S(2)}, u32[]{:S(2)}) collective-permute-start(bf16[64,5120]{1,0:T(8,128)(2,1)S(1)} %fusion.24.refs_0_.rows_ref), channel_id=1, source_target_pairs={{16,17},{17,18},{18,19},{19,16},{20,21},{21,22},{22,23},{23,20},{2... | collective-permute-start | bytes 1966088 | tf_op jit(solution)/shard_map/ppermute | solution.py:40
  198.1 15.0 %collective-permute-done.25.rows_ref.other_ref = bf16[64,5120]{1,0:T(8,128)(2,1)S(1)} collective-permute-done((bf16[64,5120]{1,0:T(8,128)(2,1)S(1)}, bf16[64,5120]{1,0:T(8,128)(2,1)S(1)}, u32[]{:S(2)}, u32[]{:S(2)}) %collective-permute-start.25) | collective-permute-done | bytes 655392 | tf_op jit(solution)/shard_map/ppermute | solution.py:38
  214.5 12.6 %collective-permute-done.22.rows_ref = bf16[64,5120]{1,0:T(8,128)(2,1)S(1)} collective-permute-done((bf16[64,5120]{1,0:T(8,128)(2,1)S(1)}, bf16[64,5120]{1,0:T(8,128)(2,1)S(1)}, u32[]{:S(2)}, u32[]{:S(2)}) %collective-permute-start.22) | collective-permute-done | bytes 655392 | tf_op jit(solution)/shard_map/ppermute | solution.py:40
  241.6 13.5 %collective-permute-done.23.rows_ref = bf16[64,5120]{1,0:T(8,128)(2,1)S(1)} collective-permute-done((bf16[64,5120]{1,0:T(8,128)(2,1)S(1)}, bf16[64,5120]{1,0:T(8,128)(2,1)S(1)}, u32[]{:S(2)}, u32[]{:S(2)}) %collective-permute-start.23) | collective-permute-done | bytes 655392 | tf_op jit(solution)/shard_map/ppermute | solution.py:40
  262.3 6.9 %collective-permute-done.31.rows_ref.other_ref = bf16[64,5120]{1,0:T(8,128)(2,1)S(1)} collective-permute-done((bf16[64,5120]{1,0:T(8,128)(2,1)S(1)}, bf16[64,5120]{1,0:T(8,128)(2,1)S(1)}, u32[]{:S(2)}, u32[]{:S(2)}) %collective-permute-start.31) | collective-permute-done | bytes 655392 | tf_op jit(solution)/shard_map/ppermute | solution.py:38
  272.0 8.4 %collective-permute-done.24.rows_ref = bf16[64,5120]{1,0:T(8,128)(2,1)S(1)} collective-permute-done((bf16[64,5120]{1,0:T(8,128)(2,1)S(1)}, bf16[64,5120]{1,0:T(8,128)(2,1)S(1)}, u32[]{:S(2)}, u32[]{:S(2)}) %collective-permute-start.24) | collective-permute-done | bytes 655392 | tf_op jit(solution)/shard_map/ppermute | solution.py:40
  (213 shorter events, 96.7 us)
Async XLA Ops:
  0.6 21.1 %collective-permute-start.1 = (bf16[1280,640]{1,0:T(8,128)(2,1)}, bf16[1280,640]{1,0:T(8,128)(2,1)}, u32[]{:S(2)}, u32[]{:S(2)}) collective-permute-start(bf16[1280,640]{1,0:T(8,128)(2,1)} %bitcast.130), channel_id=1, source_target_pairs={{0,4},{4,0},{8,12},{12,8},{1,5},{5,1},{9,13},{13,9},{2,6},{6,2},{1... | collective-permute-start | bytes 4915208 | tf_op jit(solution)/shard_map/ppermute | solution.py:38
  0.7 40.5 %collective-permute-start.5 = (bf16[1280,640]{1,0:T(8,128)(2,1)}, bf16[1280,640]{1,0:T(8,128)(2,1)}, u32[]{:S(2)}, u32[]{:S(2)}) collective-permute-start(bf16[1280,640]{1,0:T(8,128)(2,1)} %bitcast.131), channel_id=1, source_target_pairs={{16,24},{20,28},{24,16},{28,20},{17,25},{21,29},{25,17},{29,21},{1... | collective-permute-start | bytes 4915208 | tf_op jit(solution)/shard_map/ppermute | solution.py:40
  6.0 20.1 %collective-permute-start = (bf16[256,2560]{1,0:T(8,128)(2,1)}, bf16[256,2560]{1,0:T(8,128)(2,1)}, u32[]{:S(2)}, u32[]{:S(2)}) collective-permute-start(bf16[256,2560]{1,0:T(8,128)(2,1)} %dynamic-slice_bitcast_fusion), channel_id=1, source_target_pairs={{0,8},{4,12},{8,0},{12,4},{1,9},{5,13},{9,1},{13,5},{2,10},{6,14},... | collective-permute-start | bytes 3932168 | tf_op jit(solution)/shard_map/ppermute | solution.py:40
  8.5 17.6 %collective-permute-start.3 = (f32[1,256]{1,0:T(1,128)S(1)}, f32[1,256]{1,0:T(1,128)S(1)}, u32[]{:S(2)}, u32[]{:S(2)}) collective-permute-start(f32[1,256]{1,0:T(1,128)S(1)} %bitcast.143), channel_id=1, source_target_pairs={{0,8},{4,12},{8,0},{12,4},{1,9},{5,13},{9,1},{13,5},{2,10},{6,14},... | collective-permute-start | bytes 3080 | tf_op jit(solution)/shard_map/ppermute | solution.py:40
  41.3 40.2 %collective-permute-start.7 = (bf16[1280,640]{1,0:T(8,128)(2,1)S(1)}, bf16[1280,640]{1,0:T(8,128)(2,1)}, u32[]{:S(2)}, u32[]{:S(2)}) collective-permute-start(bf16[1280,640]{1,0:T(8,128)(2,1)S(1)} %bitcast.133), channel_id=1, source_target_pairs={{16,24},{20,28},{24,16},{28,20},{17,25},{21,29},{25,17},{29,21},{1... | collective-permute-start | bytes 4915208 | tf_op jit(solution)/shard_map/ppermute | solution.py:40
  43.7 37.8 %collective-permute-start.6 = (bf16[2,256,640]{2,1,0:T(8,128)(2,1)S(1)}, bf16[2,256,640]{2,1,0:T(8,128)(2,1)S(1)}, u32[]{:S(2)}, u32[]{:S(2)}) collective-permute-start(bf16[2,256,640]{2,1,0:T(8,128)(2,1)S(1)} %fusion.33), channel_id=1, source_target_pairs={{0,16},{1,17},{2,18},{3,19},{4,20},{5,21},{6,22},{7,23},{8,24},{9,... | collective-permute-start | bytes 1966088 | tf_op jit(solution)/shard_map/ppermute | solution.py:288
  97.0 16.3 %collective-permute-start.16 = (bf16[2,256,640]{2,1,0:T(8,128)(2,1)S(1)}, bf16[2,256,640]{2,1,0:T(8,128)(2,1)S(1)}, u32[]{:S(2)}, u32[]{:S(2)}) collective-permute-start(bf16[2,256,640]{2,1,0:T(8,128)(2,1)S(1)} %bitcast.125), channel_id=1, source_target_pairs={{16,8},{20,12},{24,0},{28,4},{17,9},{21,13},{25,1},{29,5},{18,10},... | collective-permute-start | bytes 1966088 | tf_op jit(solution)/shard_map/ppermute | solution.py:54
  98.3 28.6 %collective-permute-start.15 = (bf16[2,256,640]{2,1,0:T(8,128)(2,1)S(1)}, bf16[2,256,640]{2,1,0:T(8,128)(2,1)S(1)}, u32[]{:S(2)}, u32[]{:S(2)}) collective-permute-start(bf16[2,256,640]{2,1,0:T(8,128)(2,1)S(1)} %bitcast.126), channel_id=1, source_target_pairs={{16,0},{20,4},{24,8},{28,12},{17,1},{21,5},{25,9},{29,13},{18,2},{... | collective-permute-start | bytes 1966088 | tf_op jit(solution)/shard_map/ppermute | solution.py:54
  99.7 30.4 %collective-permute-start.11 = (bf16[2,64,2560]{2,1,0:T(8,128)(2,1)S(1)}, bf16[2,64,2560]{2,1,0:T(8,128)(2,1)S(1)}, u32[]{:S(2)}, u32[]{:S(2)}) collective-permute-start(bf16[2,64,2560]{2,1,0:T(8,128)(2,1)S(1)} %fusion.41.refs_0_), channel_id=1, source_target_pairs={{16,17},{17,18},{18,19},{19,16},{20,21},{21,22},{22,23},{23,20},{2... | collective-permute-start | bytes 1966088 | tf_op jit(solution)/shard_map/ppermute | solution.py:40
  106.4 28.0 %collective-permute-start.10 = (bf16[2,64,2560]{2,1,0:T(8,128)(2,1)S(1)}, bf16[2,64,2560]{2,1,0:T(8,128)(2,1)S(1)}, u32[]{:S(2)}, u32[]{:S(2)}) collective-permute-start(bf16[2,64,2560]{2,1,0:T(8,128)(2,1)S(1)} %fusion.42.refs_0_), channel_id=1, source_target_pairs={{16,17},{17,18},{18,19},{19,16},{20,21},{21,22},{22,23},{23,20},{2... | collective-permute-start | bytes 1966088 | tf_op jit(solution)/shard_map/ppermute | solution.py:40
  130.5 21.5 %collective-permute-start.13 = (bf16[2,64,2560]{2,1,0:T(8,128)(2,1)S(1)}, bf16[2,64,2560]{2,1,0:T(8,128)(2,1)S(1)}, u32[]{:S(2)}, u32[]{:S(2)}) collective-permute-start(bf16[2,64,2560]{2,1,0:T(8,128)(2,1)S(1)} %add_block.9.refs_0_.refs_4_), channel_id=1, source_target_pairs={{16,17},{17,18},{18,19},{19,16},{20,21},{21,22},{22,23},{23,20},{2... | collective-permute-start | bytes 1966088 | tf_op jit(solution)/shard_map/ppermute | solution.py:40
  134.7 31.3 %collective-permute-start.12 = (bf16[2,64,2560]{2,1,0:T(8,128)(2,1)S(1)}, bf16[2,64,2560]{2,1,0:T(8,128)(2,1)S(1)}, u32[]{:S(2)}, u32[]{:S(2)}) collective-permute-start(bf16[2,64,2560]{2,1,0:T(8,128)(2,1)S(1)} %add_block.10.refs_0_), channel_id=1, source_target_pairs={{16,17},{17,18},{18,19},{19,16},{20,21},{21,22},{22,23},{23,20},{2... | collective-permute-start | bytes 1966088 | tf_op jit(solution)/shard_map/ppermute | solution.py:40
  138.5 94.9 %collective-permute-start.30 = (bf16[256,6400]{1,0:T(8,128)(2,1)S(1)}, bf16[256,6400]{1,0:T(8,128)(2,1)S(1)}, u32[]{:S(2)}, u32[]{:S(2)}) collective-permute-start(bf16[256,6400]{1,0:T(8,128)(2,1)S(1)} %join.1), channel_id=1, source_target_pairs={{16,24},{20,28},{24,16},{28,20},{17,25},{21,29},{25,17},{29,21},{1... | collective-permute-start | bytes 9830408 | tf_op jit(solution)/shard_map/ppermute | solution.py:40
  142.0 26.3 %collective-permute-start.18 = (bf16[2,64,2560]{2,1,0:T(8,128)(2,1)S(1)}, bf16[2,64,2560]{2,1,0:T(8,128)(2,1)S(1)}, u32[]{:S(2)}, u32[]{:S(2)}) collective-permute-start(bf16[2,64,2560]{2,1,0:T(8,128)(2,1)S(1)} %add_block.13), channel_id=1, source_target_pairs={{0,1},{1,2},{2,3},{3,0},{4,5},{5,6},{6,7},{7,4},{8,9},{9,10},{10,1... | collective-permute-start | bytes 1966088 | tf_op jit(solution)/shard_map/ppermute | solution.py:40
  152.3 27.7 %collective-permute-start.20 = (bf16[2,64,2560]{2,1,0:T(8,128)(2,1)S(1)}, bf16[2,64,2560]{2,1,0:T(8,128)(2,1)S(1)}, u32[]{:S(2)}, u32[]{:S(2)}) collective-permute-start(bf16[2,64,2560]{2,1,0:T(8,128)(2,1)S(1)} %add_block.11.refs_0_), channel_id=1, source_target_pairs={{16,17},{17,18},{18,19},{19,16},{20,21},{21,22},{22,23},{23,20},{2... | collective-permute-start | bytes 1966088 | tf_op jit(solution)/shard_map/ppermute | solution.py:40
  166.4 27.2 %collective-permute-start.14 = (bf16[2,64,2560]{2,1,0:T(8,128)(2,1)S(1)}, bf16[2,64,2560]{2,1,0:T(8,128)(2,1)S(1)}, u32[]{:S(2)}, u32[]{:S(2)}) collective-permute-start(bf16[2,64,2560]{2,1,0:T(8,128)(2,1)S(1)} %add_block.12.refs_0_), channel_id=1, source_target_pairs={{16,17},{17,18},{18,19},{19,16},{20,21},{21,22},{22,23},{23,20},{2... | collective-permute-start | bytes 1966088 | tf_op jit(solution)/shard_map/ppermute | solution.py:40
  193.6 19.5 %collective-permute-start.25 = (bf16[64,5120]{1,0:T(8,128)(2,1)S(1)}, bf16[64,5120]{1,0:T(8,128)(2,1)S(1)}, u32[]{:S(2)}, u32[]{:S(2)}) collective-permute-start(bf16[64,5120]{1,0:T(8,128)(2,1)S(1)} %fusion.22.refs_0_.rows_ref.other_ref), channel_id=1, source_target_pairs={{0,1},{1,2},{2,3},{3,0},{4,5},{5,6},{6,7},{7,4},{8,9},{9,10},{10,1... | collective-permute-start | bytes 1966088 | tf_op jit(solution)/shard_map/ppermute | solution.py:38
  194.3 32.8 %collective-permute-start.22 = (bf16[64,5120]{1,0:T(8,128)(2,1)S(1)}, bf16[64,5120]{1,0:T(8,128)(2,1)S(1)}, u32[]{:S(2)}, u32[]{:S(2)}) collective-permute-start(bf16[64,5120]{1,0:T(8,128)(2,1)S(1)} %fusion.24.refs_0_.rows_ref), channel_id=1, source_target_pairs={{16,17},{17,18},{18,19},{19,16},{20,21},{21,22},{22,23},{23,20},{2... | collective-permute-start | bytes 1966088 | tf_op jit(solution)/shard_map/ppermute | solution.py:40
  213.1 28.1 %collective-permute-start.26 = (bf16[64,5120]{1,0:T(8,128)(2,1)S(1)}, bf16[64,5120]{1,0:T(8,128)(2,1)S(1)}, u32[]{:S(2)}, u32[]{:S(2)}) collective-permute-start(bf16[64,5120]{1,0:T(8,128)(2,1)S(1)} %collective-permute-done.25.rows_ref.other_ref), channel_id=1, source_target_pairs={{0,1},{1,2},{2,3},{3,0},{4,5},{5,6},{6,7},{7,4},{8,9},{9,10},{10,1... | collective-permute-start | bytes 1966088 | tf_op jit(solution)/shard_map/ppermute | solution.py:38
  227.1 28.1 %collective-permute-start.23 = (bf16[64,5120]{1,0:T(8,128)(2,1)S(1)}, bf16[64,5120]{1,0:T(8,128)(2,1)S(1)}, u32[]{:S(2)}, u32[]{:S(2)}) collective-permute-start(bf16[64,5120]{1,0:T(8,128)(2,1)S(1)} %collective-permute-done.22.rows_ref), channel_id=1, source_target_pairs={{16,17},{17,18},{18,19},{19,16},{20,21},{21,22},{22,23},{23,20},{2... | collective-permute-start | bytes 1966088 | tf_op jit(solution)/shard_map/ppermute | solution.py:40
  239.3 21.8 %collective-permute-start.33 = (bf16[2,1280,640]{2,1,0:T(8,128)(2,1)S(1)}, bf16[2,1280,640]{2,1,0:T(8,128)(2,1)S(1)}, u32[]{:S(2)}, u32[]{:S(2)}) collective-permute-start(bf16[2,1280,640]{2,1,0:T(8,128)(2,1)S(1)} %pad_maximum_fusion.4.refs_2_), channel_id=1, source_target_pairs={{0,4},{4,0},{8,12},{12,8},{1,5},{5,1},{9,13},{13,9},{2,6},{6,2},{1... | collective-permute-start | bytes 9830408 | tf_op jit(solution)/shard_map/ppermute | solution.py:38
  241.1 17.7 %collective-permute-start.32 = (f32[1,2560]{1,0:T(1,128)S(1)}, f32[1,2560]{1,0:T(1,128)S(1)}, u32[]{:S(2)}, u32[]{:S(2)}) collective-permute-start(f32[1,2560]{1,0:T(1,128)S(1)} %constant_dynamic-slice_fusion.2), channel_id=1, source_target_pairs={{0,8},{4,12},{8,0},{12,4},{1,9},{5,13},{9,1},{13,5},{2,10},{6,14},... | collective-permute-start | bytes 30728 | tf_op jit(solution)/shard_map/ppermute | solution.py:38
  241.6 27.6 %collective-permute-start.31 = (bf16[64,5120]{1,0:T(8,128)(2,1)S(1)}, bf16[64,5120]{1,0:T(8,128)(2,1)S(1)}, u32[]{:S(2)}, u32[]{:S(2)}) collective-permute-start(bf16[64,5120]{1,0:T(8,128)(2,1)S(1)} %collective-permute-done.26.refs_0_.rows_ref.other_ref), channel_id=1, source_target_pairs={{0,1},{1,2},{2,3},{3,0},{4,5},{5,6},{6,7},{7,4},{8,9},{9,10},{10,1... | collective-permute-start | bytes 1966088 | tf_op jit(solution)/shard_map/ppermute | solution.py:38
  255.2 25.1 %collective-permute-start.24 = (bf16[64,5120]{1,0:T(8,128)(2,1)S(1)}, bf16[64,5120]{1,0:T(8,128)(2,1)S(1)}, u32[]{:S(2)}, u32[]{:S(2)}) collective-permute-start(bf16[64,5120]{1,0:T(8,128)(2,1)S(1)} %collective-permute-done.23.rows_ref), channel_id=1, source_target_pairs={{16,17},{17,18},{18,19},{19,16},{20,21},{21,22},{22,23},{23,20},{2... | collective-permute-start | bytes 1966088 | tf_op jit(solution)/shard_map/ppermute | solution.py:40
  (50 other events, 247.4 us)

commit v2 on v1

--- a/solution.py
+++ b/solution.py
@@ -392,6 +392,7 @@
     out_got = send_out(out_held)
     arrivals = [(out_held, back_held)]
 
+    own_out_rows = out_held
     decoder, always = ~encoder, jnp.bool_(True)
 
     def place_grad(whole, rows, step, *before):
@@ -417,8 +418,6 @@
     arrived = out_got
     out_got = send_out(arrived)
     result, token = place_out(None, arrived, 1, token)
-    grad_states, token = place_grad(grad_states, back_held, 0, token)
-    result, token = place_out(result, out_held, 0, token)
     for part in gain_parts:
         gain_part = gain_part + part
     gain_part = pass_on(gain_part, back_got)
@@ -456,6 +455,8 @@
     first_sum, second_sum = weight_grads(core)
     first_sum = first_sum + swapped[0].astype(F32)
     second_sum = second_sum + swapped[1].astype(F32)
+    grad_states, token = place_grad(grad_states, grad_rows, 0, token)
+    result, token = place_out(result, own_out_rows, 0, token)
     back_got, out_got, grad_states, result, token = next_round(
         last, back_got, out_got, grad_states, result, token, [gain_chip, first_sum], [second_sum]
     )

time: 284 us -> 293 us (1.032)
  waiting for transfers between devices: 152 us -> 161 us
    ppermute x13, waiting for transfers between devices: 26.9 us -> 36.6 us  [permute(): return lax.ppermute(x, axis, [(i, to(i, n)) for i in range(n)])]
  transfers between devices with their start and end apart: 35 -> 35, of which waited for: 15 -> 15; matrix products, arithmetic and copies ran while one was open for 17% -> 16% of each run, Pallas kernels for 5% -> 5%
where the time goes in v2:
time: 293 us; the launch traced here: 292 us
  waiting for transfers between devices  161 us (55%)
  starting transfers between devices  48.8 us (17%)
  matrix products  25.3 us (9%)
  other arithmetic  24.1 us (8%)
  Pallas kernels  20.7 us (7%)
  local copies, waits for them, and re-layouts  9.48 us (3%)
    ppermute x19, waiting for transfers between devices, permute(): return lax.ppermute(x, ('section', axis), pairs)  111 us
    ppermute x19, starting transfers between devices, permute(): return lax.ppermute(x, ('section', axis), pairs)  39.8 us
    ppermute x13, waiting for transfers between devices, permute(): return lax.ppermute(x, axis, [(i, to(i, n)) for i in range(n)])  36.6 us
    ppermute x2, waiting for transfers between devices, home_shift(): return lax.ppermute(x, ('section', 'dp'), pairs)  14.1 us
    pallas_call x8, Pallas kernels, place_block(): pl.pallas_call(place_kernel, grid_spec=pltpu.PrefetchScalarGridSpec(num_s...  12.2 us
    dot_general x6, matrix products, dot_plain(): return jnp.dot(left, right, preferred_element_type=F32)  10.6 us
    dot_general x8, matrix products, dot_last(): lax.dot_general(left, right, (((1,), (1,)), ((), ())), preferred_element_...  9.69 us
    select_n x4, other arithmetic, in_order(): ahead = [jnp.where(core == 0, a, b) for a, b in zip(own, other)]  8.41 us
  transfers between devices with their start and end apart: 35, of which 15 were waited for; matrix products, arithmetic and copies ran while one was open for 16% of the time, Pallas kernels for 5%

profile of v2, /device:TPU:6, one launch (start us, length us, event | category | flops | bytes accessed | tf_op | source)
XLA Modules:
  0.0 292.0 jit_solution(15630743041288047285)
XLA Ops:
  17.8 2.7 broadcast_select_fusion.5
  26.6 2.6 fusion.38
  32.8 8.5 %collective-permute-done.5 = bf16[1280,640]{1,0:T(8,128)(2,1)} collective-permute-done((bf16[1280,640]{1,0:T(8,128)(2,1)}, bf16[1280,640]{1,0:T(8,128)(2,1)}, u32[]{:S(2)}, u32[]{:S(2)}) %collective-permute-start.5) | collective-permute-done | bytes 1638432 | tf_op jit(solution)/shard_map/ppermute | solution.py:40
  48.9 32.6 %collective-permute-done.7 = bf16[1280,640]{1,0:T(8,128)(2,1)} collective-permute-done((bf16[1280,640]{1,0:T(8,128)(2,1)S(1)}, bf16[1280,640]{1,0:T(8,128)(2,1)}, u32[]{:S(2)}, u32[]{:S(2)}) %collective-permute-start.7) | collective-permute-done | bytes 1638432 | tf_op jit(solution)/shard_map/ppermute | solution.py:40
  82.1 3.2 %collective-permute-done.9 = bf16[1280,640]{1,0:T(8,128)(2,1)} collective-permute-done((bf16[1280,640]{1,0:T(8,128)(2,1)}, bf16[1280,640]{1,0:T(8,128)(2,1)}, u32[]{:S(2)}, u32[]{:S(2)}) %collective-permute-start.9) | collective-permute-done | bytes 1638432 | tf_op jit(solution)/shard_map/ppermute | solution.py:38
  88.8 4.9 %attention.1 = (bf16[256,640]{1,0:T(8,128)(2,1)S(1)}, bf16[256,640]{1,0:T(8,128)(2,1)S(1)}, bf16[2,256,640]{2,1,0:T(8,128)(2,1)S(1)}) custom-call(s32[1,2]{1,0:T(1,128)S(1)} %copy-done.2, bf16[256,640]{1,0:T(8,128)(2,1)S(1)} %copy-done.5, bf16[2,256,640]{2,1,0:T(8,128)(2,1)S(1)} %collective-permute-done.6.kv_ref, bf16[256,640]{1,0:T(8,128)(2,1)S(1)} %fusion.36.g_ref), custom_call_target="tpu_custom_call" | custom-call | flops 587202560 | bytes 2621440 | tf_op jit(solution)/shard_map/attention/pallas_call | solution.py:205
  99.7 3.5 %collective-permute-start.11 = (bf16[2,64,2560]{2,1,0:T(8,128)(2,1)S(1)}, bf16[2,64,2560]{2,1,0:T(8,128)(2,1)S(1)}, u32[]{:S(2)}, u32[]{:S(2)}) collective-permute-start(bf16[2,64,2560]{2,1,0:T(8,128)(2,1)S(1)} %fusion.41.refs_0_), channel_id=1, source_target_pairs={{16,17},{17,18},{18,19},{19,16},{20,21},{21,22},{22,23},{23,20},{2... | collective-permute-start | bytes 1966088 | tf_op jit(solution)/shard_map/ppermute | solution.py:40
  106.4 3.5 %collective-permute-start.10 = (bf16[2,64,2560]{2,1,0:T(8,128)(2,1)S(1)}, bf16[2,64,2560]{2,1,0:T(8,128)(2,1)S(1)}, u32[]{:S(2)}, u32[]{:S(2)}) collective-permute-start(bf16[2,64,2560]{2,1,0:T(8,128)(2,1)S(1)} %fusion.42.refs_0_), channel_id=1, source_target_pairs={{16,17},{17,18},{18,19},{19,16},{20,21},{21,22},{22,23},{23,20},{2... | collective-permute-start | bytes 1966088 | tf_op jit(solution)/shard_map/ppermute | solution.py:40
  110.4 3.0 %collective-permute-done.16 = bf16[2,256,640]{2,1,0:T(8,128)(2,1)S(1)} collective-permute-done((bf16[2,256,640]{2,1,0:T(8,128)(2,1)S(1)}, bf16[2,256,640]{2,1,0:T(8,128)(2,1)S(1)}, u32[]{:S(2)}, u32[]{:S(2)}) %collective-permute-start.16) | collective-permute-done | bytes 655392 | tf_op jit(solution)/shard_map/ppermute | solution.py:54
  115.8 11.1 %collective-permute-done.15 = bf16[2,256,640]{2,1,0:T(8,128)(2,1)S(1)} collective-permute-done((bf16[2,256,640]{2,1,0:T(8,128)(2,1)S(1)}, bf16[2,256,640]{2,1,0:T(8,128)(2,1)S(1)}, u32[]{:S(2)}, u32[]{:S(2)}) %collective-permute-start.15) | collective-permute-done | bytes 655392 | tf_op jit(solution)/shard_map/ppermute | solution.py:54
  130.5 3.8 %collective-permute-start.13 = (bf16[2,64,2560]{2,1,0:T(8,128)(2,1)S(1)}, bf16[2,64,2560]{2,1,0:T(8,128)(2,1)S(1)}, u32[]{:S(2)}, u32[]{:S(2)}) collective-permute-start(bf16[2,64,2560]{2,1,0:T(8,128)(2,1)S(1)} %add_block.9.refs_0_.refs_4_), channel_id=1, source_target_pairs={{16,17},{17,18},{18,19},{19,16},{20,21},{21,22},{22,23},{23,20},{2... | collective-permute-start | bytes 1966088 | tf_op jit(solution)/shard_map/ppermute | solution.py:40
  134.7 3.5 %collective-permute-start.12 = (bf16[2,64,2560]{2,1,0:T(8,128)(2,1)S(1)}, bf16[2,64,2560]{2,1,0:T(8,128)(2,1)S(1)}, u32[]{:S(2)}, u32[]{:S(2)}) collective-permute-start(bf16[2,64,2560]{2,1,0:T(8,128)(2,1)S(1)} %add_block.10.refs_0_), channel_id=1, source_target_pairs={{16,17},{17,18},{18,19},{19,16},{20,21},{21,22},{22,23},{23,20},{2... | collective-permute-start | bytes 1966088 | tf_op jit(solution)/shard_map/ppermute | solution.py:40
  138.5 2.7 collective-permute-start.30
  142.7 9.3 %collective-permute-done.13.got_ref = bf16[2,64,2560]{2,1,0:T(8,128)(2,1)S(1)} collective-permute-done((bf16[2,64,2560]{2,1,0:T(8,128)(2,1)S(1)}, bf16[2,64,2560]{2,1,0:T(8,128)(2,1)S(1)}, u32[]{:S(2)}, u32[]{:S(2)}) %collective-permute-start.13) | collective-permute-done | bytes 655392 | tf_op jit(solution)/shard_map/ppermute | solution.py:40
  154.2 11.8 %collective-permute-done.12.got_ref = bf16[2,64,2560]{2,1,0:T(8,128)(2,1)S(1)} collective-permute-done((bf16[2,64,2560]{2,1,0:T(8,128)(2,1)S(1)}, bf16[2,64,2560]{2,1,0:T(8,128)(2,1)S(1)}, u32[]{:S(2)}, u32[]{:S(2)}) %collective-permute-start.12) | collective-permute-done | bytes 655392 | tf_op jit(solution)/shard_map/ppermute | solution.py:40
  169.4 10.7 %collective-permute-done.20.got_ref = bf16[2,64,2560]{2,1,0:T(8,128)(2,1)S(1)} collective-permute-done((bf16[2,64,2560]{2,1,0:T(8,128)(2,1)S(1)}, bf16[2,64,2560]{2,1,0:T(8,128)(2,1)S(1)}, u32[]{:S(2)}, u32[]{:S(2)}) %collective-permute-start.20) | collective-permute-done | bytes 655392 | tf_op jit(solution)/shard_map/ppermute | solution.py:40
  189.7 3.8 %collective-permute-done.14.got_ref = bf16[2,64,2560]{2,1,0:T(8,128)(2,1)S(1)} collective-permute-done((bf16[2,64,2560]{2,1,0:T(8,128)(2,1)S(1)}, bf16[2,64,2560]{2,1,0:T(8,128)(2,1)S(1)}, u32[]{:S(2)}, u32[]{:S(2)}) %collective-permute-start.14) | collective-permute-done | bytes 655392 | tf_op jit(solution)/shard_map/ppermute | solution.py:40
  194.3 3.7 %collective-permute-start.22 = (bf16[64,5120]{1,0:T(8,128)(2,1)S(1)}, bf16[64,5120]{1,0:T(8,128)(2,1)S(1)}, u32[]{:S(2)}, u32[]{:S(2)}) collective-permute-start(bf16[64,5120]{1,0:T(8,128)(2,1)S(1)} %fusion.24.refs_0_.rows_ref), channel_id=1, source_target_pairs={{16,17},{17,18},{18,19},{19,16},{20,21},{21,22},{22,23},{23,20},{2... | collective-permute-start | bytes 1966088 | tf_op jit(solution)/shard_map/ppermute | solution.py:40
  198.1 15.0 %collective-permute-done.25.rows_ref.other_ref = bf16[64,5120]{1,0:T(8,128)(2,1)S(1)} collective-permute-done((bf16[64,5120]{1,0:T(8,128)(2,1)S(1)}, bf16[64,5120]{1,0:T(8,128)(2,1)S(1)}, u32[]{:S(2)}, u32[]{:S(2)}) %collective-permute-start.25) | collective-permute-done | bytes 655392 | tf_op jit(solution)/shard_map/ppermute | solution.py:38
  213.1 14.0 %collective-permute-done.22.rows_ref = bf16[64,5120]{1,0:T(8,128)(2,1)S(1)} collective-permute-done((bf16[64,5120]{1,0:T(8,128)(2,1)S(1)}, bf16[64,5120]{1,0:T(8,128)(2,1)S(1)}, u32[]{:S(2)}, u32[]{:S(2)}) %collective-permute-start.22) | collective-permute-done | bytes 655392 | tf_op jit(solution)/shard_map/ppermute | solution.py:40
  237.9 3.3 %collective-permute-done.26.refs_0_.rows_ref.other_ref = bf16[64,5120]{1,0:T(8,128)(2,1)S(1)} collective-permute-done((bf16[64,5120]{1,0:T(8,128)(2,1)S(1)}, bf16[64,5120]{1,0:T(8,128)(2,1)S(1)}, u32[]{:S(2)}, u32[]{:S(2)}) %collective-permute-start.26) | collective-permute-done | bytes 655392 | tf_op jit(solution)/shard_map/ppermute | solution.py:38
  243.1 9.1 %collective-permute-done.23.rows_ref = bf16[64,5120]{1,0:T(8,128)(2,1)S(1)} collective-permute-done((bf16[64,5120]{1,0:T(8,128)(2,1)S(1)}, bf16[64,5120]{1,0:T(8,128)(2,1)S(1)}, u32[]{:S(2)}, u32[]{:S(2)}) %collective-permute-start.23) | collective-permute-done | bytes 655392 | tf_op jit(solution)/shard_map/ppermute | solution.py:40
  260.9 15.2 %collective-permute-done.31.rows_ref.other_ref = bf16[64,5120]{1,0:T(8,128)(2,1)S(1)} collective-permute-done((bf16[64,5120]{1,0:T(8,128)(2,1)S(1)}, bf16[64,5120]{1,0:T(8,128)(2,1)S(1)}, u32[]{:S(2)}, u32[]{:S(2)}) %collective-permute-start.31) | collective-permute-done | bytes 655392 | tf_op jit(solution)/shard_map/ppermute | solution.py:38
  278.9 10.9 %collective-permute-done.24.rows_ref = bf16[64,5120]{1,0:T(8,128)(2,1)S(1)} collective-permute-done((bf16[64,5120]{1,0:T(8,128)(2,1)S(1)}, bf16[64,5120]{1,0:T(8,128)(2,1)S(1)}, u32[]{:S(2)}, u32[]{:S(2)}) %collective-permute-start.24) | collective-permute-done | bytes 655392 | tf_op jit(solution)/shard_map/ppermute | solution.py:40
  (213 shorter events, 97.6 us)
Async XLA Ops:
  0.6 21.1 %collective-permute-start.1 = (bf16[1280,640]{1,0:T(8,128)(2,1)}, bf16[1280,640]{1,0:T(8,128)(2,1)}, u32[]{:S(2)}, u32[]{:S(2)}) collective-permute-start(bf16[1280,640]{1,0:T(8,128)(2,1)} %bitcast.130), channel_id=1, source_target_pairs={{0,4},{4,0},{8,12},{12,8},{1,5},{5,1},{9,13},{13,9},{2,6},{6,2},{1... | collective-permute-start | bytes 4915208 | tf_op jit(solution)/shard_map/ppermute | solution.py:38
  0.7 40.5 %collective-permute-start.5 = (bf16[1280,640]{1,0:T(8,128)(2,1)}, bf16[1280,640]{1,0:T(8,128)(2,1)}, u32[]{:S(2)}, u32[]{:S(2)}) collective-permute-start(bf16[1280,640]{1,0:T(8,128)(2,1)} %bitcast.131), channel_id=1, source_target_pairs={{16,24},{20,28},{24,16},{28,20},{17,25},{21,29},{25,17},{29,21},{1... | collective-permute-start | bytes 4915208 | tf_op jit(solution)/shard_map/ppermute | solution.py:40
  3.3 14.5 %collective-permute-start.2 = (bf16[1280,640]{1,0:T(8,128)(2,1)}, bf16[1280,640]{1,0:T(8,128)(2,1)}, u32[]{:S(2)}, u32[]{:S(2)}) collective-permute-start(bf16[1280,640]{1,0:T(8,128)(2,1)} %bitcast.132), channel_id=1, source_target_pairs={{0,4},{4,0},{8,12},{12,8},{1,5},{5,1},{9,13},{13,9},{2,6},{6,2},{1... | collective-permute-start | bytes 4915208 | tf_op jit(solution)/shard_map/ppermute | solution.py:38
  6.0 20.1 %collective-permute-start = (bf16[256,2560]{1,0:T(8,128)(2,1)}, bf16[256,2560]{1,0:T(8,128)(2,1)}, u32[]{:S(2)}, u32[]{:S(2)}) collective-permute-start(bf16[256,2560]{1,0:T(8,128)(2,1)} %dynamic-slice_bitcast_fusion), channel_id=1, source_target_pairs={{0,8},{4,12},{8,0},{12,4},{1,9},{5,13},{9,1},{13,5},{2,10},{6,14},... | collective-permute-start | bytes 3932168 | tf_op jit(solution)/shard_map/ppermute | solution.py:40
  8.5 17.6 %collective-permute-start.3 = (f32[1,256]{1,0:T(1,128)S(1)}, f32[1,256]{1,0:T(1,128)S(1)}, u32[]{:S(2)}, u32[]{:S(2)}) collective-permute-start(f32[1,256]{1,0:T(1,128)S(1)} %bitcast.143), channel_id=1, source_target_pairs={{0,8},{4,12},{8,0},{12,4},{1,9},{5,13},{9,1},{13,5},{2,10},{6,14},... | collective-permute-start | bytes 3080 | tf_op jit(solution)/shard_map/ppermute | solution.py:40
  41.3 40.2 %collective-permute-start.7 = (bf16[1280,640]{1,0:T(8,128)(2,1)S(1)}, bf16[1280,640]{1,0:T(8,128)(2,1)}, u32[]{:S(2)}, u32[]{:S(2)}) collective-permute-start(bf16[1280,640]{1,0:T(8,128)(2,1)S(1)} %bitcast.133), channel_id=1, source_target_pairs={{16,24},{20,28},{24,16},{28,20},{17,25},{21,29},{25,17},{29,21},{1... | collective-permute-start | bytes 4915208 | tf_op jit(solution)/shard_map/ppermute | solution.py:40
  43.7 37.8 %collective-permute-start.6 = (bf16[2,256,640]{2,1,0:T(8,128)(2,1)S(1)}, bf16[2,256,640]{2,1,0:T(8,128)(2,1)S(1)}, u32[]{:S(2)}, u32[]{:S(2)}) collective-permute-start(bf16[2,256,640]{2,1,0:T(8,128)(2,1)S(1)} %fusion.33), channel_id=1, source_target_pairs={{0,16},{1,17},{2,18},{3,19},{4,20},{5,21},{6,22},{7,23},{8,24},{9,... | collective-permute-start | bytes 1966088 | tf_op jit(solution)/shard_map/ppermute | solution.py:288
  97.0 16.3 %collective-permute-start.16 = (bf16[2,256,640]{2,1,0:T(8,128)(2,1)S(1)}, bf16[2,256,640]{2,1,0:T(8,128)(2,1)S(1)}, u32[]{:S(2)}, u32[]{:S(2)}) collective-permute-start(bf16[2,256,640]{2,1,0:T(8,128)(2,1)S(1)} %bitcast.125), channel_id=1, source_target_pairs={{16,8},{20,12},{24,0},{28,4},{17,9},{21,13},{25,1},{29,5},{18,10},... | collective-permute-start | bytes 1966088 | tf_op jit(solution)/shard_map/ppermute | solution.py:54
  98.3 28.6 %collective-permute-start.15 = (bf16[2,256,640]{2,1,0:T(8,128)(2,1)S(1)}, bf16[2,256,640]{2,1,0:T(8,128)(2,1)S(1)}, u32[]{:S(2)}, u32[]{:S(2)}) collective-permute-start(bf16[2,256,640]{2,1,0:T(8,128)(2,1)S(1)} %bitcast.126), channel_id=1, source_target_pairs={{16,0},{20,4},{24,8},{28,12},{17,1},{21,5},{25,9},{29,13},{18,2},{... | collective-permute-start | bytes 1966088 | tf_op jit(solution)/shard_map/ppermute | solution.py:54
  99.7 30.4 %collective-permute-start.11 = (bf16[2,64,2560]{2,1,0:T(8,128)(2,1)S(1)}, bf16[2,64,2560]{2,1,0:T(8,128)(2,1)S(1)}, u32[]{:S(2)}, u32[]{:S(2)}) collective-permute-start(bf16[2,64,2560]{2,1,0:T(8,128)(2,1)S(1)} %fusion.41.refs_0_), channel_id=1, source_target_pairs={{16,17},{17,18},{18,19},{19,16},{20,21},{21,22},{22,23},{23,20},{2... | collective-permute-start | bytes 1966088 | tf_op jit(solution)/shard_map/ppermute | solution.py:40
  106.4 28.0 %collective-permute-start.10 = (bf16[2,64,2560]{2,1,0:T(8,128)(2,1)S(1)}, bf16[2,64,2560]{2,1,0:T(8,128)(2,1)S(1)}, u32[]{:S(2)}, u32[]{:S(2)}) collective-permute-start(bf16[2,64,2560]{2,1,0:T(8,128)(2,1)S(1)} %fusion.42.refs_0_), channel_id=1, source_target_pairs={{16,17},{17,18},{18,19},{19,16},{20,21},{21,22},{22,23},{23,20},{2... | collective-permute-start | bytes 1966088 | tf_op jit(solution)/shard_map/ppermute | solution.py:40
  130.5 21.5 %collective-permute-start.13 = (bf16[2,64,2560]{2,1,0:T(8,128)(2,1)S(1)}, bf16[2,64,2560]{2,1,0:T(8,128)(2,1)S(1)}, u32[]{:S(2)}, u32[]{:S(2)}) collective-permute-start(bf16[2,64,2560]{2,1,0:T(8,128)(2,1)S(1)} %add_block.9.refs_0_.refs_4_), channel_id=1, source_target_pairs={{16,17},{17,18},{18,19},{19,16},{20,21},{21,22},{22,23},{23,20},{2... | collective-permute-start | bytes 1966088 | tf_op jit(solution)/shard_map/ppermute | solution.py:40
  134.7 31.3 %collective-permute-start.12 = (bf16[2,64,2560]{2,1,0:T(8,128)(2,1)S(1)}, bf16[2,64,2560]{2,1,0:T(8,128)(2,1)S(1)}, u32[]{:S(2)}, u32[]{:S(2)}) collective-permute-start(bf16[2,64,2560]{2,1,0:T(8,128)(2,1)S(1)} %add_block.10.refs_0_), channel_id=1, source_target_pairs={{16,17},{17,18},{18,19},{19,16},{20,21},{21,22},{22,23},{23,20},{2... | collective-permute-start | bytes 1966088 | tf_op jit(solution)/shard_map/ppermute | solution.py:40
  138.5 93.5 %collective-permute-start.30 = (bf16[256,6400]{1,0:T(8,128)(2,1)S(1)}, bf16[256,6400]{1,0:T(8,128)(2,1)S(1)}, u32[]{:S(2)}, u32[]{:S(2)}) collective-permute-start(bf16[256,6400]{1,0:T(8,128)(2,1)S(1)} %join.1), channel_id=1, source_target_pairs={{16,24},{20,28},{24,16},{28,20},{17,25},{21,29},{25,17},{29,21},{1... | collective-permute-start | bytes 9830408 | tf_op jit(solution)/shard_map/ppermute | solution.py:40
  142.0 26.3 %collective-permute-start.18 = (bf16[2,64,2560]{2,1,0:T(8,128)(2,1)S(1)}, bf16[2,64,2560]{2,1,0:T(8,128)(2,1)S(1)}, u32[]{:S(2)}, u32[]{:S(2)}) collective-permute-start(bf16[2,64,2560]{2,1,0:T(8,128)(2,1)S(1)} %add_block.13), channel_id=1, source_target_pairs={{0,1},{1,2},{2,3},{3,0},{4,5},{5,6},{6,7},{7,4},{8,9},{9,10},{10,1... | collective-permute-start | bytes 1966088 | tf_op jit(solution)/shard_map/ppermute | solution.py:40
  152.3 27.7 %collective-permute-start.20 = (bf16[2,64,2560]{2,1,0:T(8,128)(2,1)S(1)}, bf16[2,64,2560]{2,1,0:T(8,128)(2,1)S(1)}, u32[]{:S(2)}, u32[]{:S(2)}) collective-permute-start(bf16[2,64,2560]{2,1,0:T(8,128)(2,1)S(1)} %add_block.11.refs_0_), channel_id=1, source_target_pairs={{16,17},{17,18},{18,19},{19,16},{20,21},{21,22},{22,23},{23,20},{2... | collective-permute-start | bytes 1966088 | tf_op jit(solution)/shard_map/ppermute | solution.py:40
  166.4 27.2 %collective-permute-start.14 = (bf16[2,64,2560]{2,1,0:T(8,128)(2,1)S(1)}, bf16[2,64,2560]{2,1,0:T(8,128)(2,1)S(1)}, u32[]{:S(2)}, u32[]{:S(2)}) collective-permute-start(bf16[2,64,2560]{2,1,0:T(8,128)(2,1)S(1)} %add_block.12.refs_0_), channel_id=1, source_target_pairs={{16,17},{17,18},{18,19},{19,16},{20,21},{21,22},{22,23},{23,20},{2... | collective-permute-start | bytes 1966088 | tf_op jit(solution)/shard_map/ppermute | solution.py:40
  193.6 19.5 %collective-permute-start.25 = (bf16[64,5120]{1,0:T(8,128)(2,1)S(1)}, bf16[64,5120]{1,0:T(8,128)(2,1)S(1)}, u32[]{:S(2)}, u32[]{:S(2)}) collective-permute-start(bf16[64,5120]{1,0:T(8,128)(2,1)S(1)} %fusion.22.refs_0_.rows_ref.other_ref), channel_id=1, source_target_pairs={{0,1},{1,2},{2,3},{3,0},{4,5},{5,6},{6,7},{7,4},{8,9},{9,10},{10,1... | collective-permute-start | bytes 1966088 | tf_op jit(solution)/shard_map/ppermute | solution.py:38
  194.3 32.8 %collective-permute-start.22 = (bf16[64,5120]{1,0:T(8,128)(2,1)S(1)}, bf16[64,5120]{1,0:T(8,128)(2,1)S(1)}, u32[]{:S(2)}, u32[]{:S(2)}) collective-permute-start(bf16[64,5120]{1,0:T(8,128)(2,1)S(1)} %fusion.24.refs_0_.rows_ref), channel_id=1, source_target_pairs={{16,17},{17,18},{18,19},{19,16},{20,21},{21,22},{22,23},{23,20},{2... | collective-permute-start | bytes 1966088 | tf_op jit(solution)/shard_map/ppermute | solution.py:40
  213.1 28.1 %collective-permute-start.26 = (bf16[64,5120]{1,0:T(8,128)(2,1)S(1)}, bf16[64,5120]{1,0:T(8,128)(2,1)S(1)}, u32[]{:S(2)}, u32[]{:S(2)}) collective-permute-start(bf16[64,5120]{1,0:T(8,128)(2,1)S(1)} %collective-permute-done.25.rows_ref.other_ref), channel_id=1, source_target_pairs={{0,1},{1,2},{2,3},{3,0},{4,5},{5,6},{6,7},{7,4},{8,9},{9,10},{10,1... | collective-permute-start | bytes 1966088 | tf_op jit(solution)/shard_map/ppermute | solution.py:38
  227.1 25.1 %collective-permute-start.23 = (bf16[64,5120]{1,0:T(8,128)(2,1)S(1)}, bf16[64,5120]{1,0:T(8,128)(2,1)S(1)}, u32[]{:S(2)}, u32[]{:S(2)}) collective-permute-start(bf16[64,5120]{1,0:T(8,128)(2,1)S(1)} %collective-permute-done.22.rows_ref), channel_id=1, source_target_pairs={{16,17},{17,18},{18,19},{19,16},{20,21},{21,22},{22,23},{23,20},{2... | collective-permute-start | bytes 1966088 | tf_op jit(solution)/shard_map/ppermute | solution.py:40
  237.8 21.8 %collective-permute-start.33 = (bf16[2,1280,640]{2,1,0:T(8,128)(2,1)S(1)}, bf16[2,1280,640]{2,1,0:T(8,128)(2,1)S(1)}, u32[]{:S(2)}, u32[]{:S(2)}) collective-permute-start(bf16[2,1280,640]{2,1,0:T(8,128)(2,1)S(1)} %pad_maximum_fusion.4.refs_2_), channel_id=1, source_target_pairs={{0,4},{4,0},{8,12},{12,8},{1,5},{5,1},{9,13},{13,9},{2,6},{6,2},{1... | collective-permute-start | bytes 9830408 | tf_op jit(solution)/shard_map/ppermute | solution.py:38
  256.8 19.4 %collective-permute-start.31 = (bf16[64,5120]{1,0:T(8,128)(2,1)S(1)}, bf16[64,5120]{1,0:T(8,128)(2,1)S(1)}, u32[]{:S(2)}, u32[]{:S(2)}) collective-permute-start(bf16[64,5120]{1,0:T(8,128)(2,1)S(1)} %collective-permute-done.26.refs_0_.rows_ref.other_ref), channel_id=1, source_target_pairs={{0,1},{1,2},{2,3},{3,0},{4,5},{5,6},{6,7},{7,4},{8,9},{9,10},{10,1... | collective-permute-start | bytes 1966088 | tf_op jit(solution)/shard_map/ppermute | solution.py:38
  256.8 33.0 %collective-permute-start.24 = (bf16[64,5120]{1,0:T(8,128)(2,1)S(1)}, bf16[64,5120]{1,0:T(8,128)(2,1)S(1)}, u32[]{:S(2)}, u32[]{:S(2)}) collective-permute-start(bf16[64,5120]{1,0:T(8,128)(2,1)S(1)} %collective-permute-done.23.rows_ref), channel_id=1, source_target_pairs={{16,17},{17,18},{18,19},{19,16},{20,21},{21,22},{22,23},{23,20},{2... | collective-permute-start | bytes 1966088 | tf_op jit(solution)/shard_map/ppermute | solution.py:40
  (50 other events, 260.0 us)

commit v3 on v1

--- a/solution.py
+++ b/solution.py
@@ -445,7 +445,7 @@
     swapped = core_swap(halves)
     for step in range(2, last):
         back_got, out_got, grad_states, result, token = next_round(
-            step, back_got, out_got, grad_states, result, token, [gain_part], [halves]
+            step, back_got, out_got, grad_states, result, token, [gain_part], []
         )
     for part in gain_far:
         gain_chip = gain_chip + part
@@ -457,7 +457,7 @@
     first_sum = first_sum + swapped[0].astype(F32)
     second_sum = second_sum + swapped[1].astype(F32)
     back_got, out_got, grad_states, result, token = next_round(
-        last, back_got, out_got, grad_states, result, token, [gain_chip, first_sum], [second_sum]
+        last, back_got, out_got, grad_states, result, token, [gain_chip, halves, first_sum], [second_sum]
     )
     return (
         result[None, None],

time: 284 us -> 284 us (level)
  no operation moved by 1% of the time
where the time goes in v3:
time: 284 us; the launch traced here: 283 us
  waiting for transfers between devices  152 us (54%)
  starting transfers between devices  48.7 us (17%)
  matrix products  25.3 us (9%)
  other arithmetic  24.1 us (8%)
  Pallas kernels  20.7 us (7%)
  local copies, waits for them, and re-layouts  9.5 us (3%)
    ppermute x19, waiting for transfers between devices, permute(): return lax.ppermute(x, ('section', axis), pairs)  111 us
    ppermute x19, starting transfers between devices, permute(): return lax.ppermute(x, ('section', axis), pairs)  39.8 us
    ppermute x13, waiting for transfers between devices, permute(): return lax.ppermute(x, axis, [(i, to(i, n)) for i in range(n)])  26.9 us
    ppermute x2, waiting for transfers between devices, home_shift(): return lax.ppermute(x, ('section', 'dp'), pairs)  14.1 us
    pallas_call x8, Pallas kernels, place_block(): pl.pallas_call(place_kernel, grid_spec=pltpu.PrefetchScalarGridSpec(num_s...  12.2 us
    dot_general x6, matrix products, dot_plain(): return jnp.dot(left, right, preferred_element_type=F32)  10.6 us
    dot_general x8, matrix products, dot_last(): lax.dot_general(left, right, (((1,), (1,)), ((), ())), preferred_element_...  9.69 us
    select_n x4, other arithmetic, in_order(): ahead = [jnp.where(core == 0, a, b) for a, b in zip(own, other)]  8.41 us
  transfers between devices with their start and end apart: 35, of which 15 were waited for; matrix products, arithmetic and copies ran while one was open for 17% of the time, Pallas kernels for 5%

profile of v3, /device:TPU:6, one launch (start us, length us, event | category | flops | bytes accessed | tf_op | source)
XLA Modules:
  0.0 282.6 jit_solution(9376019671557551797)
XLA Ops:
  17.8 2.7 broadcast_select_fusion.5
  26.6 2.6 fusion.38
  29.2 2.6 fusion.39
  32.8 8.5 %collective-permute-done.5 = bf16[1280,640]{1,0:T(8,128)(2,1)} collective-permute-done((bf16[1280,640]{1,0:T(8,128)(2,1)}, bf16[1280,640]{1,0:T(8,128)(2,1)}, u32[]{:S(2)}, u32[]{:S(2)}) %collective-permute-start.5) | collective-permute-done | bytes 1638432 | tf_op jit(solution)/shard_map/ppermute | solution.py:40
  48.9 32.6 %collective-permute-done.7 = bf16[1280,640]{1,0:T(8,128)(2,1)} collective-permute-done((bf16[1280,640]{1,0:T(8,128)(2,1)S(1)}, bf16[1280,640]{1,0:T(8,128)(2,1)}, u32[]{:S(2)}, u32[]{:S(2)}) %collective-permute-start.7) | collective-permute-done | bytes 1638432 | tf_op jit(solution)/shard_map/ppermute | solution.py:40
  82.1 3.2 %collective-permute-done.9 = bf16[1280,640]{1,0:T(8,128)(2,1)} collective-permute-done((bf16[1280,640]{1,0:T(8,128)(2,1)}, bf16[1280,640]{1,0:T(8,128)(2,1)}, u32[]{:S(2)}, u32[]{:S(2)}) %collective-permute-start.9) | collective-permute-done | bytes 1638432 | tf_op jit(solution)/shard_map/ppermute | solution.py:38
  88.8 4.9 %attention.1 = (bf16[256,640]{1,0:T(8,128)(2,1)S(1)}, bf16[256,640]{1,0:T(8,128)(2,1)S(1)}, bf16[2,256,640]{2,1,0:T(8,128)(2,1)S(1)}) custom-call(s32[1,2]{1,0:T(1,128)S(1)} %copy-done.2, bf16[256,640]{1,0:T(8,128)(2,1)S(1)} %copy-done.5, bf16[2,256,640]{2,1,0:T(8,128)(2,1)S(1)} %collective-permute-done.6.kv_ref, bf16[256,640]{1,0:T(8,128)(2,1)S(1)} %fusion.36.g_ref), custom_call_target="tpu_custom_call" | custom-call | flops 587202560 | bytes 2621440 | tf_op jit(solution)/shard_map/attention/pallas_call | solution.py:205
  99.7 3.5 %collective-permute-start.11 = (bf16[2,64,2560]{2,1,0:T(8,128)(2,1)S(1)}, bf16[2,64,2560]{2,1,0:T(8,128)(2,1)S(1)}, u32[]{:S(2)}, u32[]{:S(2)}) collective-permute-start(bf16[2,64,2560]{2,1,0:T(8,128)(2,1)S(1)} %fusion.41.refs_0_), channel_id=1, source_target_pairs={{16,17},{17,18},{18,19},{19,16},{20,21},{21,22},{22,23},{23,20},{2... | collective-permute-start | bytes 1966088 | tf_op jit(solution)/shard_map/ppermute | solution.py:40
  106.4 3.5 %collective-permute-start.10 = (bf16[2,64,2560]{2,1,0:T(8,128)(2,1)S(1)}, bf16[2,64,2560]{2,1,0:T(8,128)(2,1)S(1)}, u32[]{:S(2)}, u32[]{:S(2)}) collective-permute-start(bf16[2,64,2560]{2,1,0:T(8,128)(2,1)S(1)} %fusion.42.refs_0_), channel_id=1, source_target_pairs={{16,17},{17,18},{18,19},{19,16},{20,21},{21,22},{22,23},{23,20},{2... | collective-permute-start | bytes 1966088 | tf_op jit(solution)/shard_map/ppermute | solution.py:40
  110.4 3.0 %collective-permute-done.16 = bf16[2,256,640]{2,1,0:T(8,128)(2,1)S(1)} collective-permute-done((bf16[2,256,640]{2,1,0:T(8,128)(2,1)S(1)}, bf16[2,256,640]{2,1,0:T(8,128)(2,1)S(1)}, u32[]{:S(2)}, u32[]{:S(2)}) %collective-permute-start.16) | collective-permute-done | bytes 655392 | tf_op jit(solution)/shard_map/ppermute | solution.py:54
  115.8 11.1 %collective-permute-done.15 = bf16[2,256,640]{2,1,0:T(8,128)(2,1)S(1)} collective-permute-done((bf16[2,256,640]{2,1,0:T(8,128)(2,1)S(1)}, bf16[2,256,640]{2,1,0:T(8,128)(2,1)S(1)}, u32[]{:S(2)}, u32[]{:S(2)}) %collective-permute-start.15) | collective-permute-done | bytes 655392 | tf_op jit(solution)/shard_map/ppermute | solution.py:54
  130.5 3.8 %collective-permute-start.13 = (bf16[2,64,2560]{2,1,0:T(8,128)(2,1)S(1)}, bf16[2,64,2560]{2,1,0:T(8,128)(2,1)S(1)}, u32[]{:S(2)}, u32[]{:S(2)}) collective-permute-start(bf16[2,64,2560]{2,1,0:T(8,128)(2,1)S(1)} %add_block.9.refs_0_.refs_4_), channel_id=1, source_target_pairs={{16,17},{17,18},{18,19},{19,16},{20,21},{21,22},{22,23},{23,20},{2... | collective-permute-start | bytes 1966088 | tf_op jit(solution)/shard_map/ppermute | solution.py:40
  134.7 3.5 %collective-permute-start.12 = (bf16[2,64,2560]{2,1,0:T(8,128)(2,1)S(1)}, bf16[2,64,2560]{2,1,0:T(8,128)(2,1)S(1)}, u32[]{:S(2)}, u32[]{:S(2)}) collective-permute-start(bf16[2,64,2560]{2,1,0:T(8,128)(2,1)S(1)} %add_block.10.refs_0_), channel_id=1, source_target_pairs={{16,17},{17,18},{18,19},{19,16},{20,21},{21,22},{22,23},{23,20},{2... | collective-permute-start | bytes 1966088 | tf_op jit(solution)/shard_map/ppermute | solution.py:40
  138.5 2.7 collective-permute-start.32
  142.7 9.3 %collective-permute-done.13.got_ref = bf16[2,64,2560]{2,1,0:T(8,128)(2,1)S(1)} collective-permute-done((bf16[2,64,2560]{2,1,0:T(8,128)(2,1)S(1)}, bf16[2,64,2560]{2,1,0:T(8,128)(2,1)S(1)}, u32[]{:S(2)}, u32[]{:S(2)}) %collective-permute-start.13) | collective-permute-done | bytes 655392 | tf_op jit(solution)/shard_map/ppermute | solution.py:40
  154.2 11.8 %collective-permute-done.12.got_ref = bf16[2,64,2560]{2,1,0:T(8,128)(2,1)S(1)} collective-permute-done((bf16[2,64,2560]{2,1,0:T(8,128)(2,1)S(1)}, bf16[2,64,2560]{2,1,0:T(8,128)(2,1)S(1)}, u32[]{:S(2)}, u32[]{:S(2)}) %collective-permute-start.12) | collective-permute-done | bytes 655392 | tf_op jit(solution)/shard_map/ppermute | solution.py:40
  169.4 10.7 %collective-permute-done.20.got_ref = bf16[2,64,2560]{2,1,0:T(8,128)(2,1)S(1)} collective-permute-done((bf16[2,64,2560]{2,1,0:T(8,128)(2,1)S(1)}, bf16[2,64,2560]{2,1,0:T(8,128)(2,1)S(1)}, u32[]{:S(2)}, u32[]{:S(2)}) %collective-permute-start.20) | collective-permute-done | bytes 655392 | tf_op jit(solution)/shard_map/ppermute | solution.py:40
  189.7 3.8 %collective-permute-done.14.got_ref = bf16[2,64,2560]{2,1,0:T(8,128)(2,1)S(1)} collective-permute-done((bf16[2,64,2560]{2,1,0:T(8,128)(2,1)S(1)}, bf16[2,64,2560]{2,1,0:T(8,128)(2,1)S(1)}, u32[]{:S(2)}, u32[]{:S(2)}) %collective-permute-start.14) | collective-permute-done | bytes 655392 | tf_op jit(solution)/shard_map/ppermute | solution.py:40
  194.3 3.7 %collective-permute-start.22 = (bf16[64,5120]{1,0:T(8,128)(2,1)S(1)}, bf16[64,5120]{1,0:T(8,128)(2,1)S(1)}, u32[]{:S(2)}, u32[]{:S(2)}) collective-permute-start(bf16[64,5120]{1,0:T(8,128)(2,1)S(1)} %fusion.24.refs_0_.rows_ref), channel_id=1, source_target_pairs={{16,17},{17,18},{18,19},{19,16},{20,21},{21,22},{22,23},{23,20},{2... | collective-permute-start | bytes 1966088 | tf_op jit(solution)/shard_map/ppermute | solution.py:40
  198.1 15.0 %collective-permute-done.25.rows_ref.other_ref = bf16[64,5120]{1,0:T(8,128)(2,1)S(1)} collective-permute-done((bf16[64,5120]{1,0:T(8,128)(2,1)S(1)}, bf16[64,5120]{1,0:T(8,128)(2,1)S(1)}, u32[]{:S(2)}, u32[]{:S(2)}) %collective-permute-start.25) | collective-permute-done | bytes 655392 | tf_op jit(solution)/shard_map/ppermute | solution.py:38
  214.5 12.6 %collective-permute-done.22.rows_ref = bf16[64,5120]{1,0:T(8,128)(2,1)S(1)} collective-permute-done((bf16[64,5120]{1,0:T(8,128)(2,1)S(1)}, bf16[64,5120]{1,0:T(8,128)(2,1)S(1)}, u32[]{:S(2)}, u32[]{:S(2)}) %collective-permute-start.22) | collective-permute-done | bytes 655392 | tf_op jit(solution)/shard_map/ppermute | solution.py:40
  241.6 13.5 %collective-permute-done.23.rows_ref = bf16[64,5120]{1,0:T(8,128)(2,1)S(1)} collective-permute-done((bf16[64,5120]{1,0:T(8,128)(2,1)S(1)}, bf16[64,5120]{1,0:T(8,128)(2,1)S(1)}, u32[]{:S(2)}, u32[]{:S(2)}) %collective-permute-start.23) | collective-permute-done | bytes 655392 | tf_op jit(solution)/shard_map/ppermute | solution.py:40
  262.3 6.9 %collective-permute-done.30.rows_ref.other_ref = bf16[64,5120]{1,0:T(8,128)(2,1)S(1)} collective-permute-done((bf16[64,5120]{1,0:T(8,128)(2,1)S(1)}, bf16[64,5120]{1,0:T(8,128)(2,1)S(1)}, u32[]{:S(2)}, u32[]{:S(2)}) %collective-permute-start.30) | collective-permute-done | bytes 655392 | tf_op jit(solution)/shard_map/ppermute | solution.py:38
  272.0 8.4 %collective-permute-done.24.rows_ref = bf16[64,5120]{1,0:T(8,128)(2,1)S(1)} collective-permute-done((bf16[64,5120]{1,0:T(8,128)(2,1)S(1)}, bf16[64,5120]{1,0:T(8,128)(2,1)S(1)}, u32[]{:S(2)}, u32[]{:S(2)}) %collective-permute-start.24) | collective-permute-done | bytes 655392 | tf_op jit(solution)/shard_map/ppermute | solution.py:40
  (213 shorter events, 96.7 us)
Async XLA Ops:
  0.6 21.1 %collective-permute-start.1 = (bf16[1280,640]{1,0:T(8,128)(2,1)}, bf16[1280,640]{1,0:T(8,128)(2,1)}, u32[]{:S(2)}, u32[]{:S(2)}) collective-permute-start(bf16[1280,640]{1,0:T(8,128)(2,1)} %bitcast.130), channel_id=1, source_target_pairs={{0,4},{4,0},{8,12},{12,8},{1,5},{5,1},{9,13},{13,9},{2,6},{6,2},{1... | collective-permute-start | bytes 4915208 | tf_op jit(solution)/shard_map/ppermute | solution.py:38
  0.7 40.5 %collective-permute-start.5 = (bf16[1280,640]{1,0:T(8,128)(2,1)}, bf16[1280,640]{1,0:T(8,128)(2,1)}, u32[]{:S(2)}, u32[]{:S(2)}) collective-permute-start(bf16[1280,640]{1,0:T(8,128)(2,1)} %bitcast.131), channel_id=1, source_target_pairs={{16,24},{20,28},{24,16},{28,20},{17,25},{21,29},{25,17},{29,21},{1... | collective-permute-start | bytes 4915208 | tf_op jit(solution)/shard_map/ppermute | solution.py:40
  6.0 20.1 %collective-permute-start = (bf16[256,2560]{1,0:T(8,128)(2,1)}, bf16[256,2560]{1,0:T(8,128)(2,1)}, u32[]{:S(2)}, u32[]{:S(2)}) collective-permute-start(bf16[256,2560]{1,0:T(8,128)(2,1)} %dynamic-slice_bitcast_fusion), channel_id=1, source_target_pairs={{0,8},{4,12},{8,0},{12,4},{1,9},{5,13},{9,1},{13,5},{2,10},{6,14},... | collective-permute-start | bytes 3932168 | tf_op jit(solution)/shard_map/ppermute | solution.py:40
  8.5 17.6 %collective-permute-start.3 = (f32[1,256]{1,0:T(1,128)S(1)}, f32[1,256]{1,0:T(1,128)S(1)}, u32[]{:S(2)}, u32[]{:S(2)}) collective-permute-start(f32[1,256]{1,0:T(1,128)S(1)} %bitcast.143), channel_id=1, source_target_pairs={{0,8},{4,12},{8,0},{12,4},{1,9},{5,13},{9,1},{13,5},{2,10},{6,14},... | collective-permute-start | bytes 3080 | tf_op jit(solution)/shard_map/ppermute | solution.py:40
  41.3 40.2 %collective-permute-start.7 = (bf16[1280,640]{1,0:T(8,128)(2,1)S(1)}, bf16[1280,640]{1,0:T(8,128)(2,1)}, u32[]{:S(2)}, u32[]{:S(2)}) collective-permute-start(bf16[1280,640]{1,0:T(8,128)(2,1)S(1)} %bitcast.133), channel_id=1, source_target_pairs={{16,24},{20,28},{24,16},{28,20},{17,25},{21,29},{25,17},{29,21},{1... | collective-permute-start | bytes 4915208 | tf_op jit(solution)/shard_map/ppermute | solution.py:40
  43.7 37.8 %collective-permute-start.6 = (bf16[2,256,640]{2,1,0:T(8,128)(2,1)S(1)}, bf16[2,256,640]{2,1,0:T(8,128)(2,1)S(1)}, u32[]{:S(2)}, u32[]{:S(2)}) collective-permute-start(bf16[2,256,640]{2,1,0:T(8,128)(2,1)S(1)} %fusion.33), channel_id=1, source_target_pairs={{0,16},{1,17},{2,18},{3,19},{4,20},{5,21},{6,22},{7,23},{8,24},{9,... | collective-permute-start | bytes 1966088 | tf_op jit(solution)/shard_map/ppermute | solution.py:288
  97.0 16.3 %collective-permute-start.16 = (bf16[2,256,640]{2,1,0:T(8,128)(2,1)S(1)}, bf16[2,256,640]{2,1,0:T(8,128)(2,1)S(1)}, u32[]{:S(2)}, u32[]{:S(2)}) collective-permute-start(bf16[2,256,640]{2,1,0:T(8,128)(2,1)S(1)} %bitcast.125), channel_id=1, source_target_pairs={{16,8},{20,12},{24,0},{28,4},{17,9},{21,13},{25,1},{29,5},{18,10},... | collective-permute-start | bytes 1966088 | tf_op jit(solution)/shard_map/ppermute | solution.py:54
  98.3 28.6 %collective-permute-start.15 = (bf16[2,256,640]{2,1,0:T(8,128)(2,1)S(1)}, bf16[2,256,640]{2,1,0:T(8,128)(2,1)S(1)}, u32[]{:S(2)}, u32[]{:S(2)}) collective-permute-start(bf16[2,256,640]{2,1,0:T(8,128)(2,1)S(1)} %bitcast.126), channel_id=1, source_target_pairs={{16,0},{20,4},{24,8},{28,12},{17,1},{21,5},{25,9},{29,13},{18,2},{... | collective-permute-start | bytes 1966088 | tf_op jit(solution)/shard_map/ppermute | solution.py:54
  99.7 30.4 %collective-permute-start.11 = (bf16[2,64,2560]{2,1,0:T(8,128)(2,1)S(1)}, bf16[2,64,2560]{2,1,0:T(8,128)(2,1)S(1)}, u32[]{:S(2)}, u32[]{:S(2)}) collective-permute-start(bf16[2,64,2560]{2,1,0:T(8,128)(2,1)S(1)} %fusion.41.refs_0_), channel_id=1, source_target_pairs={{16,17},{17,18},{18,19},{19,16},{20,21},{21,22},{22,23},{23,20},{2... | collective-permute-start | bytes 1966088 | tf_op jit(solution)/shard_map/ppermute | solution.py:40
  106.4 28.0 %collective-permute-start.10 = (bf16[2,64,2560]{2,1,0:T(8,128)(2,1)S(1)}, bf16[2,64,2560]{2,1,0:T(8,128)(2,1)S(1)}, u32[]{:S(2)}, u32[]{:S(2)}) collective-permute-start(bf16[2,64,2560]{2,1,0:T(8,128)(2,1)S(1)} %fusion.42.refs_0_), channel_id=1, source_target_pairs={{16,17},{17,18},{18,19},{19,16},{20,21},{21,22},{22,23},{23,20},{2... | collective-permute-start | bytes 1966088 | tf_op jit(solution)/shard_map/ppermute | solution.py:40
  130.5 21.5 %collective-permute-start.13 = (bf16[2,64,2560]{2,1,0:T(8,128)(2,1)S(1)}, bf16[2,64,2560]{2,1,0:T(8,128)(2,1)S(1)}, u32[]{:S(2)}, u32[]{:S(2)}) collective-permute-start(bf16[2,64,2560]{2,1,0:T(8,128)(2,1)S(1)} %add_block.9.refs_0_.refs_4_), channel_id=1, source_target_pairs={{16,17},{17,18},{18,19},{19,16},{20,21},{21,22},{22,23},{23,20},{2... | collective-permute-start | bytes 1966088 | tf_op jit(solution)/shard_map/ppermute | solution.py:40
  134.7 31.3 %collective-permute-start.12 = (bf16[2,64,2560]{2,1,0:T(8,128)(2,1)S(1)}, bf16[2,64,2560]{2,1,0:T(8,128)(2,1)S(1)}, u32[]{:S(2)}, u32[]{:S(2)}) collective-permute-start(bf16[2,64,2560]{2,1,0:T(8,128)(2,1)S(1)} %add_block.10.refs_0_), channel_id=1, source_target_pairs={{16,17},{17,18},{18,19},{19,16},{20,21},{21,22},{22,23},{23,20},{2... | collective-permute-start | bytes 1966088 | tf_op jit(solution)/shard_map/ppermute | solution.py:40
  138.5 94.9 %collective-permute-start.32 = (bf16[256,6400]{1,0:T(8,128)(2,1)S(1)}, bf16[256,6400]{1,0:T(8,128)(2,1)S(1)}, u32[]{:S(2)}, u32[]{:S(2)}) collective-permute-start(bf16[256,6400]{1,0:T(8,128)(2,1)S(1)} %join.1), channel_id=1, source_target_pairs={{16,24},{20,28},{24,16},{28,20},{17,25},{21,29},{25,17},{29,21},{1... | collective-permute-start | bytes 9830408 | tf_op jit(solution)/shard_map/ppermute | solution.py:40
  142.0 26.3 %collective-permute-start.18 = (bf16[2,64,2560]{2,1,0:T(8,128)(2,1)S(1)}, bf16[2,64,2560]{2,1,0:T(8,128)(2,1)S(1)}, u32[]{:S(2)}, u32[]{:S(2)}) collective-permute-start(bf16[2,64,2560]{2,1,0:T(8,128)(2,1)S(1)} %add_block.13), channel_id=1, source_target_pairs={{0,1},{1,2},{2,3},{3,0},{4,5},{5,6},{6,7},{7,4},{8,9},{9,10},{10,1... | collective-permute-start | bytes 1966088 | tf_op jit(solution)/shard_map/ppermute | solution.py:40
  152.3 27.7 %collective-permute-start.20 = (bf16[2,64,2560]{2,1,0:T(8,128)(2,1)S(1)}, bf16[2,64,2560]{2,1,0:T(8,128)(2,1)S(1)}, u32[]{:S(2)}, u32[]{:S(2)}) collective-permute-start(bf16[2,64,2560]{2,1,0:T(8,128)(2,1)S(1)} %add_block.11.refs_0_), channel_id=1, source_target_pairs={{16,17},{17,18},{18,19},{19,16},{20,21},{21,22},{22,23},{23,20},{2... | collective-permute-start | bytes 1966088 | tf_op jit(solution)/shard_map/ppermute | solution.py:40
  166.4 27.2 %collective-permute-start.14 = (bf16[2,64,2560]{2,1,0:T(8,128)(2,1)S(1)}, bf16[2,64,2560]{2,1,0:T(8,128)(2,1)S(1)}, u32[]{:S(2)}, u32[]{:S(2)}) collective-permute-start(bf16[2,64,2560]{2,1,0:T(8,128)(2,1)S(1)} %add_block.12.refs_0_), channel_id=1, source_target_pairs={{16,17},{17,18},{18,19},{19,16},{20,21},{21,22},{22,23},{23,20},{2... | collective-permute-start | bytes 1966088 | tf_op jit(solution)/shard_map/ppermute | solution.py:40
  193.6 19.5 %collective-permute-start.25 = (bf16[64,5120]{1,0:T(8,128)(2,1)S(1)}, bf16[64,5120]{1,0:T(8,128)(2,1)S(1)}, u32[]{:S(2)}, u32[]{:S(2)}) collective-permute-start(bf16[64,5120]{1,0:T(8,128)(2,1)S(1)} %fusion.22.refs_0_.rows_ref.other_ref), channel_id=1, source_target_pairs={{0,1},{1,2},{2,3},{3,0},{4,5},{5,6},{6,7},{7,4},{8,9},{9,10},{10,1... | collective-permute-start | bytes 1966088 | tf_op jit(solution)/shard_map/ppermute | solution.py:38
  194.3 32.8 %collective-permute-start.22 = (bf16[64,5120]{1,0:T(8,128)(2,1)S(1)}, bf16[64,5120]{1,0:T(8,128)(2,1)S(1)}, u32[]{:S(2)}, u32[]{:S(2)}) collective-permute-start(bf16[64,5120]{1,0:T(8,128)(2,1)S(1)} %fusion.24.refs_0_.rows_ref), channel_id=1, source_target_pairs={{16,17},{17,18},{18,19},{19,16},{20,21},{21,22},{22,23},{23,20},{2... | collective-permute-start | bytes 1966088 | tf_op jit(solution)/shard_map/ppermute | solution.py:40
  213.1 28.1 %collective-permute-start.26 = (bf16[64,5120]{1,0:T(8,128)(2,1)S(1)}, bf16[64,5120]{1,0:T(8,128)(2,1)S(1)}, u32[]{:S(2)}, u32[]{:S(2)}) collective-permute-start(bf16[64,5120]{1,0:T(8,128)(2,1)S(1)} %collective-permute-done.25.rows_ref.other_ref), channel_id=1, source_target_pairs={{0,1},{1,2},{2,3},{3,0},{4,5},{5,6},{6,7},{7,4},{8,9},{9,10},{10,1... | collective-permute-start | bytes 1966088 | tf_op jit(solution)/shard_map/ppermute | solution.py:38
  227.1 28.1 %collective-permute-start.23 = (bf16[64,5120]{1,0:T(8,128)(2,1)S(1)}, bf16[64,5120]{1,0:T(8,128)(2,1)S(1)}, u32[]{:S(2)}, u32[]{:S(2)}) collective-permute-start(bf16[64,5120]{1,0:T(8,128)(2,1)S(1)} %collective-permute-done.22.rows_ref), channel_id=1, source_target_pairs={{16,17},{17,18},{18,19},{19,16},{20,21},{21,22},{22,23},{23,20},{2... | collective-permute-start | bytes 1966088 | tf_op jit(solution)/shard_map/ppermute | solution.py:40
  239.3 21.8 %collective-permute-start.33 = (bf16[2,1280,640]{2,1,0:T(8,128)(2,1)S(1)}, bf16[2,1280,640]{2,1,0:T(8,128)(2,1)S(1)}, u32[]{:S(2)}, u32[]{:S(2)}) collective-permute-start(bf16[2,1280,640]{2,1,0:T(8,128)(2,1)S(1)} %pad_maximum_fusion.4.refs_3_), channel_id=1, source_target_pairs={{0,4},{4,0},{8,12},{12,8},{1,5},{5,1},{9,13},{13,9},{2,6},{6,2},{1... | collective-permute-start | bytes 9830408 | tf_op jit(solution)/shard_map/ppermute | solution.py:38
  241.1 17.7 %collective-permute-start.31 = (f32[1,2560]{1,0:T(1,128)S(1)}, f32[1,2560]{1,0:T(1,128)S(1)}, u32[]{:S(2)}, u32[]{:S(2)}) collective-permute-start(f32[1,2560]{1,0:T(1,128)S(1)} %constant_dynamic-slice_fusion.4), channel_id=1, source_target_pairs={{0,8},{4,12},{8,0},{12,4},{1,9},{5,13},{9,1},{13,5},{2,10},{6,14},... | collective-permute-start | bytes 30728 | tf_op jit(solution)/shard_map/ppermute | solution.py:38
  241.6 27.6 %collective-permute-start.30 = (bf16[64,5120]{1,0:T(8,128)(2,1)S(1)}, bf16[64,5120]{1,0:T(8,128)(2,1)S(1)}, u32[]{:S(2)}, u32[]{:S(2)}) collective-permute-start(bf16[64,5120]{1,0:T(8,128)(2,1)S(1)} %collective-permute-done.26.refs_0_.rows_ref.other_ref), channel_id=1, source_target_pairs={{0,1},{1,2},{2,3},{3,0},{4,5},{5,6},{6,7},{7,4},{8,9},{9,10},{10,1... | collective-permute-start | bytes 1966088 | tf_op jit(solution)/shard_map/ppermute | solution.py:38
  255.2 25.1 %collective-permute-start.24 = (bf16[64,5120]{1,0:T(8,128)(2,1)S(1)}, bf16[64,5120]{1,0:T(8,128)(2,1)S(1)}, u32[]{:S(2)}, u32[]{:S(2)}) collective-permute-start(bf16[64,5120]{1,0:T(8,128)(2,1)S(1)} %collective-permute-done.23.rows_ref), channel_id=1, source_target_pairs={{16,17},{17,18},{18,19},{19,16},{20,21},{21,22},{22,23},{23,20},{2... | collective-permute-start | bytes 1966088 | tf_op jit(solution)/shard_map/ppermute | solution.py:40
  (50 other events, 247.4 us)
